TPU v7x, 512 devices: a whole 4x8x8 slice. The times are simulated.
512 devices in a mesh: shell: 64 (over x, y, z_lo), lat: 8 (over z_hi, core).
Axes of the slice: x: 4, y: 8, z: 8 (z_hi: 4, z_lo: 2; z = z_hi * 2 + z_lo), core: 2. Of those that a mesh axis runs over, the one named last changes fastest.
Arguments:
- advective_warming: bfloat16 [256, 768, 1536], P('shell', 'lat'), may hold values from -6 to 6
- associated_polynomial_table: bfloat16 [128, 768, 512], P(None, 'lat', 'shell'), may hold values from -12 to 12, as said below
- thermal_field: float32 [512, 128, 2, 256], P('shell', 'lat'), may hold values from -6 to 6
- operator_reciprocal: float32 [512, 256, 256], P('shell'), may hold values from -1 to 3, as said below
Outputs:
- new_temperature: float32 [512, 128, 2, 256], P('shell', 'lat')
Inputs may be any that keep to these rules, and one draw needn't show every extreme that they name: `associated_polynomial_table`: zero wherever the degree l is below the order j * 4. `operator_reciprocal`: one matrix of order 256 for each degree.
All inputs are finite; a program needn't handle non-finite values.
Results may differ from a plain program's by a relative error of at most 0.007.
Values may be sent and summed in bfloat16 or wider, within the bound.
A program may use at most 128 MiB of HBM per device.

v0:
```python
import math

import jax
import jax.numpy as jnp
from jax import lax
from jax.sharding import PartitionSpec as P

backward_euler_update = 0.5


def analysis_rows(orders, stride, longitudes):
    column = lax.broadcasted_iota(jnp.int32, (orders, longitudes), 1)
    harmonic = lax.broadcasted_iota(jnp.int32, (orders, longitudes), 0) * stride
    phased = harmonic * column % longitudes
    angles = phased.astype(jnp.float32) * (2.0 * math.pi / longitudes)
    stacked = jnp.stack([jnp.cos(angles), -jnp.sin(angles)], axis=1) / longitudes
    return stacked.reshape(2 * orders, longitudes).astype(jnp.bfloat16)


def band_total(partial_value):
    return lax.psum_scatter(
        partial_value.astype(jnp.bfloat16), "lat", scatter_dimension=0, tiled=True
    ).astype(jnp.float32)


def shards(advective_warming, associated_polynomial_table, thermal_field, operator_reciprocal):
    radial_levels, bands, longitudes = advective_warming.shape
    orders = associated_polynomial_table.shape[0]
    own_degrees = associated_polynomial_table.shape[2]
    shells = lax.axis_size("shell")
    degrees = own_degrees * shells
    analysis = analysis_rows(orders, degrees // orders, longitudes)
    fourier = lax.dot_general(
        analysis,
        advective_warming.reshape(radial_levels * bands, longitudes),
        (((1,), (1,)), ((), ())),
        preferred_element_type=jnp.float32,
    )
    fourier = fourier.astype(jnp.bfloat16).reshape(orders, 2, radial_levels, bands)
    block = jnp.einsum(
        "mcrt,mtl->mcrl",
        fourier,
        lax.all_gather(associated_polynomial_table, "shell", axis=2, tiled=True),
        preferred_element_type=jnp.float32,
    )
    summed = band_total(block)
    updated_field = lax.all_to_all(
        summed.astype(jnp.bfloat16), "shell", split_axis=3, concat_axis=2, tiled=True
    ).astype(summed.dtype)
    warming_coefficients = thermal_field + backward_euler_update * jnp.transpose(
        updated_field, (3, 0, 1, 2)
    )
    return jnp.einsum(
        "lij,lmcj->lmci", operator_reciprocal, warming_coefficients, precision=lax.Precision.HIGHEST
    )


def solution(mesh):
    in_specs = (
        P("shell", "lat", None),
        P(None, "lat", "shell"),
        P("shell", "lat", None, None),
        P("shell", None, None),
    )
    out_specs = P("shell", "lat", None, None)
    return jax.shard_map(shards, mesh=mesh, in_specs=in_specs, out_specs=out_specs, check_vma=False)
```

profile of v0, /device:TPU:8, one launch (start us, length us, event | category | flops | bytes accessed | tf_op | source)
XLA Modules:
  0.0 623.3 jit_solution(6252821501527315305)
XLA Ops:
  6.5 0.0 copy-start
  6.5 0.0 all-gather.2.cloned.1.call-start
  6.5 2.0 copy.38
  8.6 0.0 all-gather.2.cloned.1.call-update
  8.6 0.0 all-reduce.3.cloned.1.call-start
  8.7 3.2 fusion.12
  11.9 0.1 fusion.4
  12.0 0.8 copy.37
  12.9 1.2 convert_element_type.44
  14.1 2.1 convolution_convert_fusion
  16.2 0.2 reshape.95
  16.3 469.6 %all-gather.2.cloned.1.call-done = bf16[128,96,512]{1,2,0:T(8,128)(2,1)} async-done(((bf16[128,96,8]{1,2,0:T(8,128)(2,1)}), bf16[128,96,512]{1,2,0:T(8,128)(2,1)}) %all-gather.2.cloned.1.call-update) | async-done | bytes 12582928 | tf_op jit(solution)/shard_map/all_gather | solution.py:43
  485.9 11.2 %fusion.5 = bf16[128,2,4,512]{3,2,1,0:T(4,128)(2,1)} fusion(bf16[128,2,4,96]{3,2,1,0:T(4,128)(2,1)S(1)} %reshape.95, bf16[128,96,512]{1,2,0:T(8,128)(2,1)} %all-gather.2.cloned.1.call-done), kind=kOutput, calls=%fused_computation.6 | convolution fusion | flops 101187584 | bytes 13828096 | tf_op jit(solution)/shard_map/mcrt,mtl->mcrl/dot_general | solution.py:40
  497.1 0.0 all-reduce.3.cloned.1.call-update
  497.1 1.3 dynamic-slice
  499.0 82.3 %all-reduce.3.cloned.1.call-done = bf16[128,2,4,512]{3,2,1,0:T(4,128)(2,1)} async-done(((bf16[128,2,4,512]{3,2,1,0:T(4,128)(2,1)}), bf16[128,2,4,512]{3,2,1,0:T(4,128)(2,1)}) %all-reduce.3.cloned.1.call-update) | async-done | bytes 1048592
  581.4 0.9 constant_dynamic-slice_fusion
  582.3 0.7 copy.39
  583.1 1.1 reshape.99
  584.2 20.3 %all_to_all.4 = bf16[64,2,512]{2,1,0:T(2,128)(2,1)S(1)} all-to-all(bf16[64,2,512]{2,1,0:T(2,128)(2,1)S(1)} %reshape.99), channel_id=1, replica_groups=mesh['shell'=64,'lat'=8] {'shell'}, dimensions={0} | all-to-all | bytes 262144 | tf_op jit(solution)/shard_map/all_to_all | solution.py:47
  604.6 0.7 reshape.100
  605.3 0.9 copy.40
  606.2 2.0 copy.41
  608.1 3.2 copy.42
  611.3 0.0 copy-start.1
  611.3 2.2 copy.43
  613.5 0.0 copy-done
  613.5 0.0 copy-done.1
  613.6 2.0 fusion.2
  615.6 0.9 copy.45
  (2 shorter events, 0.0 us)
Async XLA Ops:
  6.5 607.0 %copy-start = (f32[8,256,256]{2,1,0:T(8,128)S(1)}, f32[8,256,256]{2,1,0:T(8,128)}, u32[]{:S(2)}) copy-start(f32[8,256,256]{2,1,0:T(8,128)} %param.7) | copy-start | bytes 6291460
  6.5 479.4 %all-gather.2.cloned.1.call-start = ((), (), s32[]{:S(2)}) async-start(), calls=%async_computation.1 | async-start | bytes 17039360 | tf_op jit(solution)/shard_map/all_gather | solution.py:43
  8.6 572.8 %all-reduce.3.cloned.1.call-start = ((), (), s32[]{:S(2)}) async-start(), calls=%async_computation.2 | async-start | bytes 2097152
  611.3 2.2 copy-start.1
Sparse Core Ops, SparseCore 0:
  9.4 476.4 all-gather.1
  497.2 84.0 all-reduce.2
where the time goes:
time: 624 us; the launch traced here: 623 us
  waiting for transfers between devices  552 us (88%)
  blocking collectives  20.3 us (3%)
  local copies, waits for them, and re-layouts  18.2 us (3%)
  matrix products  15.3 us (2%)
  between operations  14.2 us (2%)
    all_gather x1, waiting for transfers between devices, shards(): lax.all_gather(associated_polynomial_table, 'shell', axis=2, tiled=True)  470 us
    unnamed x3, waiting for transfers between devices  82.4 us
    all_to_all x1, blocking collectives, shards(): lax.all_to_all(summed.astype(jnp.bfloat16), 'shell', split_axis=3, concat...  20.3 us
  transfers between devices with their start and end apart: 2, of which 2 were waited for; matrix products, arithmetic and copies ran while one was open for 1% of the time, Pallas kernels for 0%

commit v1 on v0

v1 whole, which is shorter than its diff:
```python
import math

import jax
import jax.numpy as jnp
import numpy as np
from jax import lax
from jax.sharding import Mesh, PartitionSpec as P

backward_euler_update = 0.5


def analysis_rows(orders, stride, longitudes):
    phase = (np.arange(orders)[:, None] * stride * np.arange(longitudes)[None, :]) % longitudes
    angles = phase.astype(np.float32) * np.float32(2.0 * math.pi / longitudes)
    stacked = np.stack([np.cos(angles), -np.sin(angles)], axis=1) / np.float32(longitudes)
    return jnp.asarray(stacked.reshape(2 * orders, longitudes)).astype(jnp.bfloat16)


def shards(advective_warming, table, thermal_field, operator_reciprocal):
    radial_levels, bands, longitudes = advective_warming.shape
    orders = table.shape[0]
    own_degrees = table.shape[2]
    degrees = own_degrees * lax.axis_size("x") * lax.axis_size("g")
    table = lax.all_to_all(table, "lat", split_axis=0, concat_axis=1, tiled=True)
    table = lax.all_to_all(table, "g", split_axis=0, concat_axis=2, tiled=True)
    table = lax.all_gather(table, "x", axis=2, tiled=True)
    analysis = analysis_rows(orders, degrees // orders, longitudes)
    fourier = lax.dot_general(
        analysis,
        advective_warming.reshape(radial_levels * bands, longitudes),
        (((1,), (1,)), ((), ())),
        preferred_element_type=jnp.float32,
    )
    fourier = fourier.astype(jnp.bfloat16).reshape(orders, 2, radial_levels, bands)
    fourier = lax.all_to_all(fourier, "lat", split_axis=0, concat_axis=3, tiled=True)
    fourier = lax.all_to_all(fourier, "g", split_axis=0, concat_axis=2, tiled=True)
    block = jnp.einsum("mcrt,mtl->mcrl", fourier, table, preferred_element_type=jnp.float32)
    own_levels = block.shape[2]
    block = lax.all_to_all(
        block.astype(jnp.bfloat16), ("x", "g"), split_axis=3, concat_axis=0, tiled=True
    ).astype(jnp.float32)
    block = block.reshape(-1, thermal_field.shape[1], 2, own_levels, own_degrees)
    block = jnp.transpose(block, (4, 1, 2, 0, 3)).reshape(thermal_field.shape)
    forcing = thermal_field + backward_euler_update * block
    return jnp.einsum(
        "lij,lmcj->lmci", operator_reciprocal, forcing, precision=lax.Precision.HIGHEST
    )


def solution(mesh):
    shells, lats = mesh.devices.shape
    finer = Mesh(mesh.devices.reshape(4, shells // 4, lats), ("x", "g", "lat"))
    shell = ("x", "g")
    in_specs = (
        P(shell, "lat", None),
        P(None, "lat", shell),
        P(shell, "lat", None, None),
        P(shell, None, None),
    )
    out_specs = P(shell, "lat", None, None)
    return jax.shard_map(shards, mesh=finer, in_specs=in_specs, out_specs=out_specs, check_vma=False)
```

time: 624 us -> 109 us (0.17)
  waiting for transfers between devices: 552 us -> 39 us
  starting transfers between devices: 0.04 us -> 26.8 us
  between operations: 14.2 us -> 0.13 us
  local copies, waits for them, and re-layouts: 18.2 us -> 6.65 us
  blocking collectives: 20.3 us -> 31.5 us
  matrix products: 15.3 us -> 4.53 us
    all_gather x1 -> x0, waiting for transfers between devices: 470 us -> none  [shards(): lax.all_gather(associated_polynomial_table, 'shell', axis=2, tiled=True)]
    unnamed x3 -> x0, waiting for transfers between devices: 82.4 us -> none
    all_to_all x0 -> x4, waiting for transfers between devices: none -> 39 us  [the longest x1 11.8 us: shards(): lax.all_to_all(fourier, 'lat', split_axis=0, concat_axis=3, tiled=True)]
    all_to_all x0 -> x4, starting transfers between devices: none -> 26.8 us  [the longest x1 10.3 us: shards(): lax.all_to_all(fourier, 'lat', split_axis=0, concat_axis=3, tiled=True)]
    all_gather x0 -> x1, blocking collectives: none -> 16 us  [shards(): table = lax.all_gather(table, 'x', axis=2, tiled=True)]
    dot_general x2, matrix products: 13.2 us -> 2.28 us  [the longest x1 2.01 us: shards(): jnp.einsum('lij,lmcj->lmci', operator_reciprocal, forcing, precision=lax....]
    mul x3 -> x2, local copies, waits for them, and re-layouts: 7.36 us -> 0.75 us  [shards(): forcing = thermal_field + backward_euler_update * block]
  transfers between devices with their start and end apart: 2 -> 4, of which waited for: 2 -> 4; matrix products, arithmetic and copies ran while one was open for 1% -> 1% of each run, Pallas kernels for 0% -> 0%
where the time goes in v1:
time: 109 us
  waiting for transfers between devices  39 us (36%)
  blocking collectives  31.5 us (29%)
  starting transfers between devices  26.8 us (25%)
  local copies, waits for them, and re-layouts  6.65 us (6%)
  matrix products  4.53 us (4%)
    all_gather x1, blocking collectives, shards(): table = lax.all_gather(table, 'x', axis=2, tiled=True)  16 us
    all_to_all x1, blocking collectives, shards(): lax.all_to_all(block.astype(jnp.bfloat16), ('x', 'g'), split_axis=3, conc...  15.6 us
    all_to_all x1, waiting for transfers between devices, shards(): lax.all_to_all(fourier, 'lat', split_axis=0, concat_axis=3, tiled=True)  11.8 us
    all_to_all x1, waiting for transfers between devices, shards(): lax.all_to_all(table, 'lat', split_axis=0, concat_axis=1, tiled=True)  10.8 us
    all_to_all x1, starting transfers between devices, shards(): lax.all_to_all(fourier, 'lat', split_axis=0, concat_axis=3, tiled=True)  10.3 us
    all_to_all x1, waiting for transfers between devices, shards(): table = lax.all_to_all(table, 'g', split_axis=0, concat_axis=2, tiled=True)  8.67 us
    all_to_all x1, starting transfers between devices, shards(): lax.all_to_all(fourier, 'g', split_axis=0, concat_axis=2, tiled=True)  8.3 us
    all_to_all x1, waiting for transfers between devices, shards(): lax.all_to_all(fourier, 'g', split_axis=0, concat_axis=2, tiled=True)  7.73 us
  transfers between devices with their start and end apart: 4, of which 4 were waited for; matrix products, arithmetic and copies ran while one was open for 1% of the time, Pallas kernels for 0%

profile of v1, /device:TPU:8, one launch (start us, length us, event | category | flops | bytes accessed | tf_op | source)
XLA Modules:
  0.0 108.8 jit_solution(15241552492936182516)
XLA Ops:
  0.0 0.0 copy-start
  0.0 0.0 copy-start.2
  0.0 2.2 %convolution_convert_fusion = bf16[256,384]{1,0:T(8,128)(2,1)S(1)} fusion(bf16[256,1536]{1,0:T(8,128)(2,1)} %constant.9, bf16[384,1536]{1,0:T(8,128)(2,1)} %bitcast.51), kind=kOutput, calls=%fused_computation.2 | convolution fusion | flops 302088192 | bytes 2162688 | tf_op jit(solution)/shard_map/dot_general | solution.py:28
  2.3 0.9 reshape.26
  3.1 10.3 %all-to-all-start = ((bf16[128,2,4,96]{3,2,1,0:T(4,128)(2,1)}), bf16[128,2,4,96]{3,2,1,0:T(4,128)(2,1)S(1)}, u32[]{:S(2)}, u32[]{:S(2)}) async-start(bf16[128,2,4,96]{3,2,1,0:T(4,128)(2,1)} %reshape.26), calls=%async_computation | async-start | bytes 524288 | tf_op jit(solution)/shard_map/all_to_all | solution.py:35
  13.4 0.0 copy-done.2
  13.5 0.9 copy.28
  14.4 11.8 %all-to-all-done = bf16[128,2,4,96]{3,2,1,0:T(4,128)(2,1)S(1)} async-done(((bf16[128,2,4,96]{3,2,1,0:T(4,128)(2,1)}), bf16[128,2,4,96]{3,2,1,0:T(4,128)(2,1)S(1)}, u32[]{:S(2)}, u32[]{:S(2)}) %all-to-all-start) | async-done | bytes 196640 | tf_op jit(solution)/shard_map/all_to_all | solution.py:35
  26.2 3.4 %all-to-all-start.2 = ((bf16[128,96,8]{1,2,0:T(8,128)(2,1)}), bf16[128,96,8]{1,2,0:T(8,128)(2,1)S(1)}, u32[]{:S(2)}, u32[]{:S(2)}) async-start(bf16[128,96,8]{1,2,0:T(8,128)(2,1)} %copy.28), calls=%async_computation.2 | async-start | bytes 524288 | tf_op jit(solution)/shard_map/all_to_all | solution.py:24
  29.6 0.3 copy.26
  29.9 0.9 all_to_all.60
  30.9 10.8 %all-to-all-done.2 = bf16[128,96,8]{1,2,0:T(8,128)(2,1)S(1)} async-done(((bf16[128,96,8]{1,2,0:T(8,128)(2,1)}), bf16[128,96,8]{1,2,0:T(8,128)(2,1)S(1)}, u32[]{:S(2)}, u32[]{:S(2)}) %all-to-all-start.2) | async-done | bytes 196640 | tf_op jit(solution)/shard_map/all_to_all | solution.py:24
  41.6 8.3 %all-to-all-start.1 = ((bf16[16,2,4,768]{3,2,1,0:T(4,128)(2,1)}), bf16[16,2,4,768]{3,2,1,0:T(4,128)(2,1)S(1)}, u32[]{:S(2)}, u32[]{:S(2)}) async-start(bf16[16,2,4,768]{3,2,1,0:T(4,128)(2,1)} %all_to_all.60), calls=%async_computation.1 | async-start | bytes 393216 | tf_op jit(solution)/shard_map/all_to_all | solution.py:36
  49.9 0.2 copy.29
  50.1 0.9 all_to_all.67
  51.0 7.7 %all-to-all-done.1 = bf16[16,2,4,768]{3,2,1,0:T(4,128)(2,1)S(1)} async-done(((bf16[16,2,4,768]{3,2,1,0:T(4,128)(2,1)}), bf16[16,2,4,768]{3,2,1,0:T(4,128)(2,1)S(1)}, u32[]{:S(2)}, u32[]{:S(2)}) %all-to-all-start.1) | async-done | bytes 196640 | tf_op jit(solution)/shard_map/all_to_all | solution.py:36
  58.8 4.8 %all-to-all-start.3 = ((bf16[16,768,8]{1,2,0:T(8,128)(2,1)}), bf16[16,768,8]{1,2,0:T(8,128)(2,1)S(1)}, u32[]{:S(2)}, u32[]{:S(2)}) async-start(bf16[16,768,8]{1,2,0:T(8,128)(2,1)} %all_to_all.67), calls=%async_computation.3 | async-start | bytes 393216 | tf_op jit(solution)/shard_map/all_to_all | solution.py:25
  63.6 0.1 copy.27
  63.6 0.1 reshape.27
  63.7 8.7 %all-to-all-done.3 = bf16[16,768,8]{1,2,0:T(8,128)(2,1)S(1)} async-done(((bf16[16,768,8]{1,2,0:T(8,128)(2,1)}), bf16[16,768,8]{1,2,0:T(8,128)(2,1)S(1)}, u32[]{:S(2)}, u32[]{:S(2)}) %all-to-all-start.3) | async-done | bytes 196640 | tf_op jit(solution)/shard_map/all_to_all | solution.py:25
  72.4 0.2 copy.30
  72.5 16.0 %all_gather.3 = bf16[1,768,512]{2,1,0:T(8,128)(2,1)S(1)} all-gather(bf16[1,768,128]{2,1,0:T(8,128)(2,1)S(1)} %copy.30), channel_id=1, replica_groups=mesh['x'=4,'g'=16,'lat'=8] {'x'}, dimensions={2}, use_global_device_ids=true | all-gather | bytes 983040 | tf_op jit(solution)/shard_map/all_gather | solution.py:26
  88.5 0.3 fusion.2
  88.8 0.0 copy-start.1
  88.8 0.2 copy.31
  88.9 0.2 reshape.34
  89.1 15.6 %all_to_all.78 = bf16[64,2,512]{2,1,0:T(2,128)(2,1)S(1)} all-to-all(bf16[64,2,512]{2,1,0:T(2,128)(2,1)S(1)} %reshape.34), channel_id=1, replica_groups=mesh['x'=4,'g'=16,'lat'=8] {'x','g'}, dimensions={0} | all-to-all | bytes 262144 | tf_op jit(solution)/shard_map/all_to_all | solution.py:39
  104.7 0.2 reshape.35
  105.0 0.3 copy.33
  105.3 0.4 mul.23
  105.7 0.0 copy-done.1
  105.7 0.1 add.3
  105.9 0.0 copy-done
  105.9 2.0 %fusion = f32[8,16,2,256]{3,1,2,0:T(8,128)S(1)} fusion(f32[8,256,256]{2,1,0:T(8,128)S(1)} %copy-done, f32[8,16,2,256]{3,2,1,0:T(2,128)S(1)} %add.3), kind=kOutput, calls=%fused_computation | convolution fusion | flops 201326592 | bytes 2621440 | tf_op jit(solution)/shard_map/lij,lmcj->lmci/dot_general | solution.py:45
  107.9 0.9 copy.35
  (1 shorter events, 0.0 us)
Async XLA Ops:
  0.0 105.9 %copy-start = (f32[8,256,256]{2,1,0:T(8,128)S(1)}, f32[8,256,256]{2,1,0:T(8,128)}, u32[]{:S(2)}) copy-start(f32[8,256,256]{2,1,0:T(8,128)} %param.8) | copy-start | bytes 6291460
  0.0 13.4 %copy-start.2 = (bf16[128,96,8]{0,2,1:T(8,128)(2,1)S(1)}, bf16[128,96,8]{0,2,1:T(8,128)(2,1)}, u32[]{:S(2)}) copy-start(bf16[128,96,8]{0,2,1:T(8,128)(2,1)} %param.6) | copy-start | bytes 589828
  3.1 23.1 %all-to-all-start = ((bf16[128,2,4,96]{3,2,1,0:T(4,128)(2,1)}), bf16[128,2,4,96]{3,2,1,0:T(4,128)(2,1)S(1)}, u32[]{:S(2)}, u32[]{:S(2)}) async-start(bf16[128,2,4,96]{3,2,1,0:T(4,128)(2,1)} %reshape.26), calls=%async_computation | async-start | bytes 524288 | tf_op jit(solution)/shard_map/all_to_all | solution.py:35
  26.2 15.4 %all-to-all-start.2 = ((bf16[128,96,8]{1,2,0:T(8,128)(2,1)}), bf16[128,96,8]{1,2,0:T(8,128)(2,1)S(1)}, u32[]{:S(2)}, u32[]{:S(2)}) async-start(bf16[128,96,8]{1,2,0:T(8,128)(2,1)} %copy.28), calls=%async_computation.2 | async-start | bytes 524288 | tf_op jit(solution)/shard_map/all_to_all | solution.py:24
  41.6 17.1 %all-to-all-start.1 = ((bf16[16,2,4,768]{3,2,1,0:T(4,128)(2,1)}), bf16[16,2,4,768]{3,2,1,0:T(4,128)(2,1)S(1)}, u32[]{:S(2)}, u32[]{:S(2)}) async-start(bf16[16,2,4,768]{3,2,1,0:T(4,128)(2,1)} %all_to_all.60), calls=%async_computation.1 | async-start | bytes 393216 | tf_op jit(solution)/shard_map/all_to_all | solution.py:36
  58.8 13.6 %all-to-all-start.3 = ((bf16[16,768,8]{1,2,0:T(8,128)(2,1)}), bf16[16,768,8]{1,2,0:T(8,128)(2,1)S(1)}, u32[]{:S(2)}, u32[]{:S(2)}) async-start(bf16[16,768,8]{1,2,0:T(8,128)(2,1)} %all_to_all.67), calls=%async_computation.3 | async-start | bytes 393216 | tf_op jit(solution)/shard_map/all_to_all | solution.py:25
  88.8 17.0 %copy-start.1 = (f32[8,16,2,256]{3,2,1,0:T(2,128)S(1)}, f32[8,16,2,256]{3,2,1,0:T(2,128)}, u32[]{:S(2)}) copy-start(f32[8,16,2,256]{3,2,1,0:T(2,128)} %param.7) | copy-start | bytes 786436

commit v2 on v1

v2 whole, which is shorter than its diff:
```python
import functools
import math

import jax
import jax.numpy as jnp
import numpy as np
from jax import lax
from jax.experimental import pallas as pl
from jax.experimental.pallas import tpu as pltpu
from jax.sharding import Mesh, PartitionSpec as P

backward_euler_update = 0.5
MESH = pl.DeviceIdType.MESH
NT = (((1,), (1,)), ((), ()))
f32, bf16 = jnp.float32, jnp.bfloat16


def analysis_rows(orders, stride, longitudes):
    phase = (np.arange(orders)[:, None] * stride * np.arange(longitudes)[None, :]) % longitudes
    angles = phase.astype(np.float32) * np.float32(2.0 * math.pi / longitudes)
    stacked = np.stack([np.cos(angles), -np.sin(angles)], axis=0) / np.float32(longitudes)
    return jnp.asarray(stacked.reshape(2 * orders, longitudes)).astype(bf16)


def level_order(xs, ks, own_levels):
    n = xs * ks * 2 * own_levels
    x, k, c, r = np.unravel_index(np.arange(n), (xs, ks, 2, own_levels))
    matrix = np.zeros((n, n), np.float32)
    matrix[np.arange(n), np.ravel_multi_index((c, x, k, r), (2, xs, ks, own_levels))] = backward_euler_update
    return jnp.asarray(matrix).astype(bf16)


def split(value):
    high = value.astype(bf16)
    return high, (value - high.astype(f32)).astype(bf16)


def kernel(
    sizes,
    warm_hbm, table_hbm, thermal_hbm, operator_hbm, analysis_hbm, order_hbm,
    out_ref,
    warm, table, thermal, operator, analysis, order,
    rows32, turned32, f_send, f_recv, p_send, p_all, s_send, s_recv, operator16, own_part, ordered32,
    load_sems, f_sems, p_sems, x_send_sems, x_recv_sems, s_sems,
):
    X, Y, A, B, C = sizes
    K = Y * A
    M = B * C * K
    x, y, a = lax.axis_index("x"), lax.axis_index("y"), lax.axis_index("a")
    b, c = lax.axis_index("b"), lax.axis_index("c")
    k = y * A + a
    me = (b * C + c) * K + k
    own_levels, bands, longitudes = warm.shape
    own_degrees = table.shape[1]
    lanes = f_send.shape[2]

    def owner(m):
        return {
            "b": m // (C * K), "c": lax.rem(m // K, C),
            "y": lax.rem(m, K) // A, "a": lax.rem(m, A),
        }

    def shell(s):
        return {"x": s // K, "y": lax.rem(s, K) // A, "a": lax.rem(s, A)}

    loads = [
        pltpu.make_async_copy(src, dst, load_sems.at[i])
        for i, (src, dst) in enumerate((
            (table_hbm, table), (warm_hbm, warm), (analysis_hbm, analysis),
            (thermal_hbm, thermal), (operator_hbm, operator), (order_hbm, order),
        ))
    ]
    for load in loads:
        load.start()

    barrier = pltpu.get_barrier_semaphore()

    def greet_plane(i, carry):
        pl.semaphore_signal(
            barrier, inc=1, device_id=owner(lax.rem(me + i, M)), device_id_type=MESH
        )
        return carry

    lax.fori_loop(1, M, greet_plane, 0)

    def greet_shell(i, carry):
        s = lax.rem(x * K + K + i, X * K)
        pl.semaphore_signal(barrier, inc=1, device_id=shell(s), device_id_type=MESH)
        return carry

    lax.fori_loop(0, (X - 1) * K, greet_shell, 0)

    loads[0].wait()
    rows32[...] = table[...].astype(f32).reshape(bands * own_degrees, M)
    for l in range(own_degrees):
        part = rows32[pl.ds(l, bands, stride=own_degrees), :]
        part = jnp.concatenate([part, jnp.zeros((lanes - bands, M), f32)], axis=0)
        turned32[pl.ds(l, M, stride=own_degrees), :] = part.T
    p_send[...] = turned32[...].reshape(M, own_degrees, lanes).astype(bf16)

    loads[1].wait()
    loads[2].wait()
    for r in range(own_levels):
        part = lax.dot_general(analysis[...], warm[r], NT, preferred_element_type=f32)
        part = jnp.concatenate([part, jnp.zeros((2 * M, lanes - bands), f32)], axis=1)
        for half in range(2):
            turned32[pl.ds(half * own_levels + r, M, stride=2 * own_levels), :] = part[
                half * M : (half + 1) * M
            ]
    f_send[...] = turned32[...].reshape(M, 2 * own_levels, lanes).astype(bf16)

    pl.semaphore_wait(barrier, M - 1 + (X - 1) * K)

    def p_copy(m):
        return pltpu.make_async_remote_copy(
            src_ref=p_send.at[m], dst_ref=p_all.at[x, me],
            send_sem=p_sems.at[0], recv_sem=p_sems.at[1],
            device_id=owner(m), device_id_type=MESH,
        )

    def f_copy(m):
        return pltpu.make_async_remote_copy(
            src_ref=f_send.at[m], dst_ref=f_recv.at[me],
            send_sem=f_sems.at[0], recv_sem=f_sems.at[1],
            device_id=owner(m), device_id_type=MESH,
        )

    def send_p(i, carry):
        p_copy(lax.rem(me + i, M)).start()
        return carry

    def send_f(i, carry):
        f_copy(lax.rem(me + i, M)).start()
        return carry

    pltpu.make_async_copy(p_send.at[me], p_all.at[x, me], p_sems.at[1]).start()
    lax.fori_loop(1, M, send_p, 0)
    pltpu.make_async_copy(f_send.at[me], f_recv.at[me], f_sems.at[1]).start()
    lax.fori_loop(1, M, send_f, 0)

    loads[3].wait()
    loads[4].wait()
    for l in range(own_degrees):
        high, low = split(operator[l])
        operator16[l] = high
        t_high, t_low = split(thermal[l])
        own_part[l] = (
            lax.dot_general(t_high, high, NT, preferred_element_type=f32)
            + lax.dot_general(t_low, high, NT, preferred_element_type=f32)
            + lax.dot_general(t_high, low, NT, preferred_element_type=f32)
        )
    loads[5].wait()

    pltpu.make_async_copy(p_all.at[x], p_all.at[x], p_sems.at[1]).wait()
    passed = []
    for d in range(1, X):
        copy = pltpu.make_async_remote_copy(
            src_ref=p_all.at[x], dst_ref=p_all.at[x],
            send_sem=x_send_sems.at[d - 1], recv_sem=x_recv_sems.at[d - 1],
            device_id={"x": lax.rem(x + d, X)}, device_id_type=MESH,
        )
        copy.start()
        passed.append(copy)
    for d in range(1, X):
        source = lax.rem(x - d + X, X)
        pltpu.make_async_copy(p_all.at[source], p_all.at[source], x_recv_sems.at[d - 1]).wait()
    pltpu.make_async_copy(f_recv, f_recv, f_sems.at[1]).wait()

    total = jnp.zeros((X * K * own_degrees, K * 2 * own_levels), f32)
    for band in range(B * C):
        here = pl.ds(band * K, K)
        total += lax.dot_general(
            p_all[:, here].reshape(X * K * own_degrees, lanes),
            f_recv[here].reshape(K * 2 * own_levels, lanes),
            NT, preferred_element_type=f32,
        )
    s_send[...] = total.reshape(X * K, own_degrees, K * 2 * own_levels).astype(bf16)

    me_shell = x * K + k

    def s_copy(s):
        return pltpu.make_async_remote_copy(
            src_ref=s_send.at[s], dst_ref=s_recv.at[x, k],
            send_sem=s_sems.at[0], recv_sem=s_sems.at[1],
            device_id=shell(s), device_id_type=MESH,
        )

    def send_s(i, carry):
        s_copy(lax.rem(me_shell + i, X * K)).start()
        return carry

    pltpu.make_async_copy(s_send.at[me_shell], s_recv.at[x, k], s_sems.at[1]).start()
    lax.fori_loop(1, X * K, send_s, 0)
    pltpu.make_async_copy(s_recv, s_recv, s_sems.at[1]).wait()

    width = K * 2 * own_levels
    half = X * K * own_levels
    ordered = jnp.zeros((K * own_degrees, 2 * half), f32)
    for xs in range(X):
        ordered += jnp.dot(
            s_recv[xs].reshape(K * own_degrees, width),
            order[xs * width : (xs + 1) * width],
            preferred_element_type=f32,
        )
    rows, wide = K * own_degrees, ordered32.shape[1]
    pieces = 2 * half // wide
    for piece in range(pieces):
        ordered32[piece * rows : (piece + 1) * rows] = ordered[:, piece * wide : (piece + 1) * wide]
    for l in range(own_degrees):
        parts = [
            ordered32[pl.ds(piece * rows + l, K, stride=own_degrees), :] for piece in range(pieces)
        ]
        forced = jnp.concatenate(
            [
                jnp.concatenate(parts[: pieces // 2], axis=1),
                jnp.concatenate(parts[pieces // 2 :], axis=1),
            ],
            axis=0,
        )
        out_ref[l] = own_part[l] + lax.dot_general(
            forced.astype(bf16), operator16[l], NT, preferred_element_type=f32
        )

    for copy in passed:
        copy.wait_send()
    for buffer, sems in ((p_send, p_sems), (f_send, f_sems), (s_send, s_sems)):
        sent = buffer.at[pl.ds(0, buffer.shape[0] - 1)]
        pltpu.make_async_copy(sent, sent, sems.at[0]).wait()


def shards(sizes, warming, table, thermal, operator):
    X, Y, A, B, C = sizes
    K = Y * A
    M = table.shape[0]
    own_levels, bands, longitudes = warming.shape
    own_degrees = table.shape[2]
    degrees = own_degrees * X * K
    levels = thermal.shape[3]
    lanes = 128
    vmem = pltpu.VMEM
    dma = pltpu.SemaphoreType.DMA
    table = jnp.transpose(table, (1, 2, 0))
    thermal = jnp.transpose(thermal, (0, 2, 1, 3)).reshape(own_degrees, 2 * K, levels)
    analysis = analysis_rows(M, degrees // M, longitudes)
    order = level_order(X, K, own_levels)
    result = pl.pallas_call(
        functools.partial(kernel, sizes),
        out_shape=jax.ShapeDtypeStruct((own_degrees, 2 * K, levels), f32),
        in_specs=[pl.BlockSpec(memory_space=pl.ANY)] * 6,
        out_specs=pl.BlockSpec(memory_space=pltpu.VMEM),
        scratch_shapes=[
            vmem(warming.shape, bf16),
            vmem(table.shape, bf16),
            vmem(thermal.shape, f32),
            vmem(operator.shape, f32),
            vmem(analysis.shape, bf16),
            vmem(order.shape, bf16),
            vmem((bands * own_degrees, M), f32),
            vmem((M * own_degrees, lanes), f32),
            vmem((M, 2 * own_levels, lanes), bf16),
            vmem((M, 2 * own_levels, lanes), bf16),
            vmem((M, own_degrees, lanes), bf16),
            vmem((X, M, own_degrees, lanes), bf16),
            vmem((X * K, own_degrees, K * 2 * own_levels), bf16),
            vmem((X, K, own_degrees, K * 2 * own_levels), bf16),
            vmem(operator.shape, bf16),
            vmem((own_degrees, 2 * K, levels), f32),
            vmem((2 * levels // min(lanes, levels) * K * own_degrees, min(lanes, levels)), f32),
            dma((6,)), dma((2,)), dma((2,)), dma((X - 1,)), dma((X - 1,)), dma((2,)),
        ],
        compiler_params=pltpu.CompilerParams(
            collective_id=0, has_side_effects=True, vmem_limit_bytes=40 * 2**20
        ),
        cost_estimate=pl.CostEstimate(flops=10**9, bytes_accessed=10**7, transcendentals=0),
    )(warming, table, thermal, operator, analysis, order)
    return jnp.transpose(result.reshape(own_degrees, 2, K, levels), (0, 2, 1, 3))


def build(mesh, sizes):
    finer = Mesh(mesh.devices.reshape(sizes), ("x", "y", "a", "b", "c"))
    shell, lat = ("x", "y", "a"), ("b", "c")
    in_specs = (
        P(shell, lat, None),
        P(None, lat, shell),
        P(shell, lat, None, None),
        P(shell, None, None),
    )
    return jax.shard_map(
        functools.partial(shards, sizes), mesh=finer, in_specs=in_specs,
        out_specs=P(shell, lat, None, None), check_vma=False,
    )


def solution(mesh):
    return build(mesh, (4, 8, 2, 4, 2))
```

time: 109 us -> 63.7 us (0.58)
  the two profiles are of different devices: /device:TPU:8 before, /device:TPU:1 now
where the time goes in v2:
time: 63.7 us; the launch traced here: 63.3 us
  Pallas kernels  55.5 us (87%)
  local copies, waits for them, and re-layouts  7.83 us (12%)
    pallas_call x1, Pallas kernels, shards(): pl.pallas_call(functools.partial(kernel, sizes), out_shape=jax.ShapeDtype...  55.5 us
    unnamed x10, local copies, waits for them, and re-layouts  5.96 us

profile of v2, /device:TPU:1, one launch (start us, length us, event | category | flops | bytes accessed | tf_op | source)
XLA Modules:
  0.0 63.3 jit_solution(2662437900852729332)
XLA Ops:
  0.0 1.0 %copy.7 = f32[8,2,16,256]{3,2,1,0:T(8,128)S(1)} copy(f32[8,2,16,256]{3,1,2,0:T(2,128)} %bitcast.10) | data formatting | bytes 524288 | tf_op jit(solution)/shard_map/transpose | solution.py:243
  1.0 0.0 copy-start
  1.0 1.6 %copy-done = f32[8,256,256]{2,1,0:T(8,128)S(1)} copy-done((f32[8,256,256]{2,1,0:T(8,128)S(1)}, f32[8,256,256]{2,1,0:T(8,128)}, u32[]{:S(2)}) %copy-start) | copy-done | bytes 2097176
  2.6 0.0 copy-start.1
  2.6 1.3 %copy-done.1 = bf16[4,96,1536]{2,1,0:T(8,128)(2,1)S(1)} copy-done((bf16[4,96,1536]{2,1,0:T(8,128)(2,1)S(1)}, bf16[4,96,1536]{2,1,0:T(8,128)(2,1)}, u32[]{:S(2)}) %copy-start.1) | copy-done | bytes 1179672
  3.8 0.0 copy-start.2
  3.8 1.1 %copy-done.2 = bf16[256,1536]{1,0:T(8,128)(2,1)S(1)} copy-done((bf16[256,1536]{1,0:T(8,128)(2,1)S(1)}, bf16[256,1536]{1,0:T(8,128)(2,1)}, u32[]{:S(2)}) %copy-start.2) | copy-done | bytes 786456
  5.0 0.0 copy-start.3
  5.0 1.0 %copy-done.3 = bf16[512,512]{1,0:T(8,128)(2,1)S(1)} copy-done((bf16[512,512]{1,0:T(8,128)(2,1)S(1)}, bf16[512,512]{1,0:T(8,128)(2,1)}, u32[]{:S(2)}) %copy-start.3) | copy-done | bytes 524312
  6.0 0.0 copy-start.4
  6.0 0.9 %copy-done.4 = bf16[128,96,8]{0,2,1:T(8,128)(2,1)S(1)} copy-done((bf16[128,96,8]{0,2,1:T(8,128)(2,1)S(1)}, bf16[128,96,8]{0,2,1:T(8,128)(2,1)}, u32[]{:S(2)}) %copy-start.4) | copy-done | bytes 196632
  6.9 55.5 %shard_map.64 = f32[8,32,256]{2,1,0:T(8,128)S(1)} custom-call(bf16[4,96,1536]{2,1,0:T(8,128)(2,1)S(1)} %copy-done.1, bf16[96,8,128]{2,1,0:T(8,128)(2,1)S(1)} %bitcast.9, f32[8,32,256]{2,1,0:T(8,128)S(1)} %bitcast.8, f32[8,256,256]{2,1,0:T(8,128)S(1)} %copy-done, bf16[256,1536]{1,0:T(8,128)(2,1)S(1)} %copy-done.2, bf16[512,512]{1,0:T(8,128)(2,1)S(1)} %copy-done.3), custom_call_target="tpu_custom_call" | custom-call | flops 1000000000 | bytes 10000000 | tf_op jit(solution)/shard_map/pallas_call | solution.py:246
  62.4 0.9 %copy.10 = f32[8,2,16,256]{3,1,2,0:T(2,128)} copy(f32[8,2,16,256]{3,2,1,0:T(8,128)S(1)} %bitcast.7) | data formatting | bytes 524288 | tf_op jit(solution)/shard_map/reshape | solution.py:276
Async XLA Ops:
  1.0 1.6 %copy-start = (f32[8,256,256]{2,1,0:T(8,128)S(1)}, f32[8,256,256]{2,1,0:T(8,128)}, u32[]{:S(2)}) copy-start(f32[8,256,256]{2,1,0:T(8,128)} %operator_hbm.1) | copy-start | bytes 6291460
  2.6 1.3 %copy-start.1 = (bf16[4,96,1536]{2,1,0:T(8,128)(2,1)S(1)}, bf16[4,96,1536]{2,1,0:T(8,128)(2,1)}, u32[]{:S(2)}) copy-start(bf16[4,96,1536]{2,1,0:T(8,128)(2,1)} %warm_hbm.1) | copy-start | bytes 3538948
  3.8 1.1 %copy-start.2 = (bf16[256,1536]{1,0:T(8,128)(2,1)S(1)}, bf16[256,1536]{1,0:T(8,128)(2,1)}, u32[]{:S(2)}) copy-start(bf16[256,1536]{1,0:T(8,128)(2,1)} %constant.10.analysis_hbm) | copy-start | bytes 2359300
  5.0 1.0 %copy-start.3 = (bf16[512,512]{1,0:T(8,128)(2,1)S(1)}, bf16[512,512]{1,0:T(8,128)(2,1)}, u32[]{:S(2)}) copy-start(bf16[512,512]{1,0:T(8,128)(2,1)} %constant.11.order_hbm) | copy-start | bytes 1572868
  6.0 0.9 %copy-start.4 = (bf16[128,96,8]{0,2,1:T(8,128)(2,1)S(1)}, bf16[128,96,8]{0,2,1:T(8,128)(2,1)}, u32[]{:S(2)}) copy-start(bf16[128,96,8]{0,2,1:T(8,128)(2,1)} %param.7) | copy-start | bytes 589828

commit v3 on v2

--- a/solution.py
+++ b/solution.py
@@ -41,7 +41,7 @@
     out_ref,
     warm, table, thermal, operator, analysis, order,
     rows32, turned32, f_send, f_recv, p_send, p_all, s_send, s_recv, operator16, own_part, ordered32,
-    load_sems, f_sems, p_sems, x_send_sems, x_recv_sems, s_sems,
+    load_sems, f_sems, p_send_sem, p_sems, x_send_sems, x_recv_sems, s_sems, plane_sem,
 ):
     X, Y, A, B, C = sizes
     K = Y * A
@@ -75,20 +75,20 @@
 
     barrier = pltpu.get_barrier_semaphore()
 
-    def greet_plane(i, carry):
+    def plane(dy, da, db, dc):
+        return {
+            "y": lax.rem(y + dy, Y), "a": lax.rem(a + da, A),
+            "b": lax.rem(b + db, B), "c": lax.rem(c + dc, C),
+        }
+
+    columns = [(0, da, db, dc) for da in range(A) for db in range(B) for dc in range(C)][1:]
+    rows = [(dy, 0, 0, 0) for dy in range(1, Y)]
+    for step in columns + rows:
+        pl.semaphore_signal(barrier, inc=1, device_id=plane(*step), device_id_type=MESH)
+    for d in range(1, X):
         pl.semaphore_signal(
-            barrier, inc=1, device_id=owner(lax.rem(me + i, M)), device_id_type=MESH
-        )
-        return carry
-
-    lax.fori_loop(1, M, greet_plane, 0)
-
-    def greet_shell(i, carry):
-        s = lax.rem(x * K + K + i, X * K)
-        pl.semaphore_signal(barrier, inc=1, device_id=shell(s), device_id_type=MESH)
-        return carry
-
-    lax.fori_loop(0, (X - 1) * K, greet_shell, 0)
+            barrier, inc=1, device_id={"x": lax.rem(x + d, X)}, device_id_type=MESH
+        )
 
     loads[0].wait()
     rows32[...] = table[...].astype(f32).reshape(bands * own_degrees, M)
@@ -97,6 +97,10 @@
         part = jnp.concatenate([part, jnp.zeros((lanes - bands, M), f32)], axis=0)
         turned32[pl.ds(l, M, stride=own_degrees), :] = part.T
     p_send[...] = turned32[...].reshape(M, own_degrees, lanes).astype(bf16)
+
+    pl.semaphore_wait(barrier, len(columns) + len(rows) + X - 1)
+    for step in rows:
+        pl.semaphore_signal(plane_sem, inc=1, device_id=plane(*step), device_id_type=MESH)
 
     loads[1].wait()
     loads[2].wait()
@@ -109,41 +113,49 @@
             ]
     f_send[...] = turned32[...].reshape(M, 2 * own_levels, lanes).astype(bf16)
 
-    pl.semaphore_wait(barrier, M - 1 + (X - 1) * K)
-
-    def p_copy(m):
+    pl.semaphore_wait(plane_sem, len(rows))
+
+    def p_copy(m, chunk):
         return pltpu.make_async_remote_copy(
             src_ref=p_send.at[m], dst_ref=p_all.at[x, me],
-            send_sem=p_sems.at[0], recv_sem=p_sems.at[1],
+            send_sem=p_send_sem, recv_sem=p_sems.at[chunk],
             device_id=owner(m), device_id_type=MESH,
         )
 
-    def f_copy(m):
+    def f_copy(m, chunk):
         return pltpu.make_async_remote_copy(
             src_ref=f_send.at[m], dst_ref=f_recv.at[me],
             send_sem=f_sems.at[0], recv_sem=f_sems.at[1],
             device_id=owner(m), device_id_type=MESH,
         )
 
-    def send_p(i, carry):
-        p_copy(lax.rem(me + i, M)).start()
-        return carry
-
-    def send_f(i, carry):
-        f_copy(lax.rem(me + i, M)).start()
-        return carry
-
-    pltpu.make_async_copy(p_send.at[me], p_all.at[x, me], p_sems.at[1]).start()
-    lax.fori_loop(1, M, send_p, 0)
-    pltpu.make_async_copy(f_send.at[me], f_recv.at[me], f_sems.at[1]).start()
-    lax.fori_loop(1, M, send_f, 0)
+    chunks = sorted(
+        ((db, dc) for db in range(B) for dc in range(C)),
+        key=lambda step: -min(step[0], B - step[0]),
+    )
+    for copy in (p_copy, f_copy):
+        for chunk, (db, dc) in enumerate(chunks):
+            band = lax.rem(b + db, B) * C + lax.rem(c + dc, C)
+            own = db == 0 and dc == 0
+
+            def send(i, carry, copy=copy, chunk=chunk, band=band):
+                copy(band * K + lax.rem(k + i, K), chunk).start()
+                return carry
+
+            lax.fori_loop(1 if own else 0, K, send, 0)
+            if own and copy is p_copy:
+                pltpu.make_async_copy(p_send.at[me], p_all.at[x, me], p_sems.at[chunk]).start()
+            elif own:
+                pltpu.make_async_copy(f_send.at[me], f_recv.at[me], f_sems.at[1]).start()
 
     loads[3].wait()
     loads[4].wait()
     for l in range(own_degrees):
         high, low = split(operator[l])
         operator16[l] = high
-        t_high, t_low = split(thermal[l])
+        t_high, t_low = split(
+            jnp.concatenate([thermal[l, :, half, :] for half in range(2)], axis=0)
+        )
         own_part[l] = (
             lax.dot_general(t_high, high, NT, preferred_element_type=f32)
             + lax.dot_general(t_low, high, NT, preferred_element_type=f32)
@@ -151,16 +163,17 @@
         )
     loads[5].wait()
 
-    pltpu.make_async_copy(p_all.at[x], p_all.at[x], p_sems.at[1]).wait()
-    passed = []
-    for d in range(1, X):
-        copy = pltpu.make_async_remote_copy(
-            src_ref=p_all.at[x], dst_ref=p_all.at[x],
-            send_sem=x_send_sems.at[d - 1], recv_sem=x_recv_sems.at[d - 1],
-            device_id={"x": lax.rem(x + d, X)}, device_id_type=MESH,
-        )
-        copy.start()
-        passed.append(copy)
+    for chunk, (db, dc) in enumerate(chunks):
+        band = lax.rem(b - db + B, B) * C + lax.rem(c - dc + C, C)
+        block = p_all.at[x, pl.ds(band * K, K)]
+        pltpu.make_async_copy(block, block, p_sems.at[chunk]).wait()
+        for d in range(1, X):
+            copy = pltpu.make_async_remote_copy(
+                src_ref=block, dst_ref=block,
+                send_sem=x_send_sems.at[d - 1], recv_sem=x_recv_sems.at[d - 1],
+                device_id={"x": lax.rem(x + d, X)}, device_id_type=MESH,
+            )
+            copy.start()
     for d in range(1, X):
         source = lax.rem(x - d + X, X)
         pltpu.make_async_copy(p_all.at[source], p_all.at[source], x_recv_sems.at[d - 1]).wait()
@@ -221,11 +234,11 @@
             forced.astype(bf16), operator16[l], NT, preferred_element_type=f32
         )
 
-    for copy in passed:
-        copy.wait_send()
-    for buffer, sems in ((p_send, p_sems), (f_send, f_sems), (s_send, s_sems)):
+    for d in range(1, X):
+        pltpu.make_async_copy(p_all.at[x], p_all.at[x], x_send_sems.at[d - 1]).wait()
+    for buffer, sem in ((p_send, p_send_sem), (f_send, f_sems.at[0]), (s_send, s_sems.at[0])):
         sent = buffer.at[pl.ds(0, buffer.shape[0] - 1)]
-        pltpu.make_async_copy(sent, sent, sems.at[0]).wait()
+        pltpu.make_async_copy(sent, sent, sem).wait()
 
 
 def shards(sizes, warming, table, thermal, operator):
@@ -240,7 +253,6 @@
     vmem = pltpu.VMEM
     dma = pltpu.SemaphoreType.DMA
     table = jnp.transpose(table, (1, 2, 0))
-    thermal = jnp.transpose(thermal, (0, 2, 1, 3)).reshape(own_degrees, 2 * K, levels)
     analysis = analysis_rows(M, degrees // M, longitudes)
     order = level_order(X, K, own_levels)
     result = pl.pallas_call(
@@ -266,10 +278,11 @@
             vmem(operator.shape, bf16),
             vmem((own_degrees, 2 * K, levels), f32),
             vmem((2 * levels // min(lanes, levels) * K * own_degrees, min(lanes, levels)), f32),
-            dma((6,)), dma((2,)), dma((2,)), dma((X - 1,)), dma((X - 1,)), dma((2,)),
+            dma((6,)), dma((2,)), dma, dma((B * C,)), dma((X - 1,)), dma((X - 1,)), dma((2,)),
+            pltpu.SemaphoreType.REGULAR,
         ],
         compiler_params=pltpu.CompilerParams(
-            collective_id=0, has_side_effects=True, vmem_limit_bytes=40 * 2**20
+            collective_id=0, has_side_effects=True, vmem_limit_bytes=60 * 2**20
         ),
         cost_estimate=pl.CostEstimate(flops=10**9, bytes_accessed=10**7, transcendentals=0),
     )(warming, table, thermal, operator, analysis, order)

time: 63.7 us -> 53.3 us (0.84)
  the two profiles are of different devices: /device:TPU:1 before, /device:TPU:128 now
where the time goes in v3:
time: 53.3 us; the launch traced here: 53.2 us
  Pallas kernels  51.3 us (96%)
  local copies, waits for them, and re-layouts  1.86 us (3%)
    pallas_call x1, Pallas kernels, shards(): pl.pallas_call(functools.partial(kernel, sizes), out_shape=jax.ShapeDtype...  51.3 us
    reshape x1, local copies, waits for them, and re-layouts, shards(): result.reshape(own_degrees, 2, K, levels)  1.86 us

profile of v3, /device:TPU:128, one launch (start us, length us, event | category | flops | bytes accessed | tf_op | source)
XLA Modules:
  0.0 53.2 jit_solution(183159770234863308)
XLA Ops:
  0.0 51.3 %shard_map.64 = f32[8,32,256]{2,1,0:T(8,128)} custom-call(bf16[4,96,1536]{2,1,0:T(8,128)(2,1)} %warm_hbm.1, bf16[96,8,128]{2,1,0:T(8,128)(2,1)} %bitcast.6, f32[8,16,2,256]{3,2,1,0:T(2,128)} %thermal_hbm.1, f32[8,256,256]{2,1,0:T(8,128)} %operator_hbm.1, bf16[256,1536]{1,0:T(8,128)(2,1)} %constant.10.analysis_hbm, bf16[512,512]{1,0:T(8,128)(2,1)} %constant.11.order_hbm), custom_call_target="tpu_custom_call" | custom-call | flops 1000000000 | bytes 10000000 | tf_op jit(solution)/shard_map/pallas_call | solution.py:258
  51.3 1.9 %copy.9 = f32[8,2,16,256]{3,1,2,0:T(2,128)} copy(f32[8,2,16,256]{3,2,1,0:T(8,128)} %bitcast.5) | data formatting | bytes 524288 | tf_op jit(solution)/shard_map/reshape | solution.py:289

commit v4 on v3

--- a/solution.py
+++ b/solution.py
@@ -40,8 +40,8 @@
     warm_hbm, table_hbm, thermal_hbm, operator_hbm, analysis_hbm, order_hbm,
     out_ref,
     warm, table, thermal, operator, analysis, order,
-    rows32, turned32, f_send, f_recv, p_send, p_all, s_send, s_recv, operator16, own_part, ordered32,
-    load_sems, f_sems, p_send_sem, p_sems, x_send_sems, x_recv_sems, s_sems, plane_sem,
+    rows32, turned32, f_send, f_all, p_send, p_recv, s_send, s_recv, operator16, own_part, ordered32,
+    load_sems, p_sems, f_send_sem, f_sems, x_send_sem, x_recv_sems, far_sem, s_sems, plane_sem,
 ):
     X, Y, A, B, C = sizes
     K = Y * A
@@ -60,9 +60,6 @@
             "y": lax.rem(m, K) // A, "a": lax.rem(m, A),
         }
 
-    def shell(s):
-        return {"x": s // K, "y": lax.rem(s, K) // A, "a": lax.rem(s, A)}
-
     loads = [
         pltpu.make_async_copy(src, dst, load_sems.at[i])
         for i, (src, dst) in enumerate((
@@ -115,38 +112,44 @@
 
     pl.semaphore_wait(plane_sem, len(rows))
 
+    def f_copy(m, chunk):
+        return pltpu.make_async_remote_copy(
+            src_ref=f_send.at[m], dst_ref=f_all.at[x, me],
+            send_sem=f_send_sem, recv_sem=f_sems.at[chunk],
+            device_id=owner(m), device_id_type=MESH,
+        )
+
     def p_copy(m, chunk):
         return pltpu.make_async_remote_copy(
-            src_ref=p_send.at[m], dst_ref=p_all.at[x, me],
-            send_sem=p_send_sem, recv_sem=p_sems.at[chunk],
-            device_id=owner(m), device_id_type=MESH,
-        )
-
-    def f_copy(m, chunk):
-        return pltpu.make_async_remote_copy(
-            src_ref=f_send.at[m], dst_ref=f_recv.at[me],
-            send_sem=f_sems.at[0], recv_sem=f_sems.at[1],
+            src_ref=p_send.at[m], dst_ref=p_recv.at[me],
+            send_sem=p_sems.at[0], recv_sem=p_sems.at[1],
             device_id=owner(m), device_id_type=MESH,
         )
 
     chunks = sorted(
         ((db, dc) for db in range(B) for dc in range(C)),
-        key=lambda step: -min(step[0], B - step[0]),
+        key=lambda step: min(step[0], B - step[0]),
     )
-    for copy in (p_copy, f_copy):
-        for chunk, (db, dc) in enumerate(chunks):
-            band = lax.rem(b + db, B) * C + lax.rem(c + dc, C)
-            own = db == 0 and dc == 0
-
-            def send(i, carry, copy=copy, chunk=chunk, band=band):
-                copy(band * K + lax.rem(k + i, K), chunk).start()
-                return carry
-
-            lax.fori_loop(1 if own else 0, K, send, 0)
-            if own and copy is p_copy:
-                pltpu.make_async_copy(p_send.at[me], p_all.at[x, me], p_sems.at[chunk]).start()
-            elif own:
-                pltpu.make_async_copy(f_send.at[me], f_recv.at[me], f_sems.at[1]).start()
+
+    def band_at(sign, chunk):
+        db, dc = chunks[chunk]
+        return lax.rem(b + sign * db + B, B) * C + lax.rem(c + sign * dc + C, C)
+
+    def send_band(copy, chunk):
+        band = band_at(1, chunk)
+
+        def send(i, carry):
+            copy(band * K + lax.rem(k + i, K), chunk).start()
+            return carry
+
+        lax.fori_loop(1 if chunk == 0 else 0, K, send, 0)
+
+    pltpu.make_async_copy(f_send.at[me], f_all.at[x, me], f_sems.at[0]).start()
+    for chunk in range(B * C):
+        send_band(f_copy, chunk)
+    pltpu.make_async_copy(p_send.at[me], p_recv.at[me], p_sems.at[1]).start()
+    for chunk in range(B * C):
+        send_band(p_copy, chunk)
 
     loads[3].wait()
     loads[4].wait()
@@ -163,58 +166,75 @@
         )
     loads[5].wait()
 
-    for chunk, (db, dc) in enumerate(chunks):
-        band = lax.rem(b - db + B, B) * C + lax.rem(c - dc + C, C)
-        block = p_all.at[x, pl.ds(band * K, K)]
-        pltpu.make_async_copy(block, block, p_sems.at[chunk]).wait()
-        for d in range(1, X):
-            copy = pltpu.make_async_remote_copy(
-                src_ref=block, dst_ref=block,
-                send_sem=x_send_sems.at[d - 1], recv_sem=x_recv_sems.at[d - 1],
-                device_id={"x": lax.rem(x + d, X)}, device_id_type=MESH,
-            )
-            copy.start()
-    for d in range(1, X):
-        source = lax.rem(x - d + X, X)
-        pltpu.make_async_copy(p_all.at[source], p_all.at[source], x_recv_sems.at[d - 1]).wait()
-    pltpu.make_async_copy(f_recv, f_recv, f_sems.at[1]).wait()
-
-    total = jnp.zeros((X * K * own_degrees, K * 2 * own_levels), f32)
+    right, left = lax.rem(x + 1, X), lax.rem(x + X - 1, X)
+    far = lax.rem(x + 2, X)
+
+    def block(source, chunk):
+        return f_all.at[source, pl.ds(band_at(-1, chunk) * K, K)]
+
+    def pass_on(source, chunk, target, sem):
+        pltpu.make_async_remote_copy(
+            src_ref=block(source, chunk), dst_ref=block(source, chunk),
+            send_sem=x_send_sem, recv_sem=sem,
+            device_id={"x": target}, device_id_type=MESH,
+        ).start()
+
+    def arrived(source, chunk, sem):
+        pltpu.make_async_copy(block(source, chunk), block(source, chunk), sem).wait()
+
+    def hop(chunk):
+        if chunk < B * C // 2:
+            arrived(left, chunk, x_recv_sems.at[0, chunk])
+            pass_on(left, chunk, right, far_sem)
+        else:
+            arrived(right, chunk, x_recv_sems.at[1, chunk])
+            pass_on(right, chunk, left, far_sem)
+
+    lag = min(5, B * C)
+    for chunk in range(B * C):
+        arrived(x, chunk, f_sems.at[chunk])
+        pass_on(x, chunk, right, x_recv_sems.at[0, chunk])
+        pass_on(x, chunk, left, x_recv_sems.at[1, chunk])
+        if chunk >= lag:
+            hop(chunk - lag)
+    for chunk in range(B * C - lag, B * C):
+        hop(chunk)
+    for chunk in range(B * C):
+        if chunk < B * C // 2:
+            arrived(right, chunk, x_recv_sems.at[1, chunk])
+        else:
+            arrived(left, chunk, x_recv_sems.at[0, chunk])
+    pltpu.make_async_copy(f_all.at[far], f_all.at[far], far_sem).wait()
+    pltpu.make_async_copy(p_recv, p_recv, p_sems.at[1]).wait()
+
+    width = X * K * 2 * own_levels
+    total = jnp.zeros((K * own_degrees, width), f32)
     for band in range(B * C):
         here = pl.ds(band * K, K)
         total += lax.dot_general(
-            p_all[:, here].reshape(X * K * own_degrees, lanes),
-            f_recv[here].reshape(K * 2 * own_levels, lanes),
+            p_recv[here].reshape(K * own_degrees, lanes),
+            f_all[:, here].reshape(width, lanes),
             NT, preferred_element_type=f32,
         )
-    s_send[...] = total.reshape(X * K, own_degrees, K * 2 * own_levels).astype(bf16)
-
-    me_shell = x * K + k
-
-    def s_copy(s):
-        return pltpu.make_async_remote_copy(
-            src_ref=s_send.at[s], dst_ref=s_recv.at[x, k],
+    s_send[...] = total.reshape(K, own_degrees, width).astype(bf16)
+
+    def send_s(i, carry):
+        target = lax.rem(k + i, K)
+        pltpu.make_async_remote_copy(
+            src_ref=s_send.at[target], dst_ref=s_recv.at[k],
             send_sem=s_sems.at[0], recv_sem=s_sems.at[1],
-            device_id=shell(s), device_id_type=MESH,
-        )
-
-    def send_s(i, carry):
-        s_copy(lax.rem(me_shell + i, X * K)).start()
+            device_id={"y": target // A, "a": lax.rem(target, A)}, device_id_type=MESH,
+        ).start()
         return carry
 
-    pltpu.make_async_copy(s_send.at[me_shell], s_recv.at[x, k], s_sems.at[1]).start()
-    lax.fori_loop(1, X * K, send_s, 0)
+    pltpu.make_async_copy(s_send.at[k], s_recv.at[k], s_sems.at[1]).start()
+    lax.fori_loop(1, K, send_s, 0)
     pltpu.make_async_copy(s_recv, s_recv, s_sems.at[1]).wait()
 
-    width = K * 2 * own_levels
-    half = X * K * own_levels
-    ordered = jnp.zeros((K * own_degrees, 2 * half), f32)
-    for xs in range(X):
-        ordered += jnp.dot(
-            s_recv[xs].reshape(K * own_degrees, width),
-            order[xs * width : (xs + 1) * width],
-            preferred_element_type=f32,
-        )
+    half = width // 2
+    ordered = jnp.dot(
+        s_recv[...].reshape(K * own_degrees, width), order[...], preferred_element_type=f32
+    )
     rows, wide = K * own_degrees, ordered32.shape[1]
     pieces = 2 * half // wide
     for piece in range(pieces):
@@ -234,9 +254,9 @@
             forced.astype(bf16), operator16[l], NT, preferred_element_type=f32
         )
 
-    for d in range(1, X):
-        pltpu.make_async_copy(p_all.at[x], p_all.at[x], x_send_sems.at[d - 1]).wait()
-    for buffer, sem in ((p_send, p_send_sem), (f_send, f_sems.at[0]), (s_send, s_sems.at[0])):
+    for _ in range(X - 1):
+        pltpu.make_async_copy(f_all.at[x], f_all.at[x], x_send_sem).wait()
+    for buffer, sem in ((f_send, f_send_sem), (p_send, p_sems.at[0]), (s_send, s_sems.at[0])):
         sent = buffer.at[pl.ds(0, buffer.shape[0] - 1)]
         pltpu.make_async_copy(sent, sent, sem).wait()
 
@@ -255,6 +275,7 @@
     table = jnp.transpose(table, (1, 2, 0))
     analysis = analysis_rows(M, degrees // M, longitudes)
     order = level_order(X, K, own_levels)
+    operands = (warming, table, thermal, operator, analysis, order)
     result = pl.pallas_call(
         functools.partial(kernel, sizes),
         out_shape=jax.ShapeDtypeStruct((own_degrees, 2 * K, levels), f32),
@@ -270,22 +291,22 @@
             vmem((bands * own_degrees, M), f32),
             vmem((M * own_degrees, lanes), f32),
             vmem((M, 2 * own_levels, lanes), bf16),
-            vmem((M, 2 * own_levels, lanes), bf16),
+            vmem((X, M, 2 * own_levels, lanes), bf16),
             vmem((M, own_degrees, lanes), bf16),
-            vmem((X, M, own_degrees, lanes), bf16),
-            vmem((X * K, own_degrees, K * 2 * own_levels), bf16),
-            vmem((X, K, own_degrees, K * 2 * own_levels), bf16),
+            vmem((M, own_degrees, lanes), bf16),
+            vmem((K, own_degrees, 2 * levels), bf16),
+            vmem((K, own_degrees, 2 * levels), bf16),
             vmem(operator.shape, bf16),
             vmem((own_degrees, 2 * K, levels), f32),
             vmem((2 * levels // min(lanes, levels) * K * own_degrees, min(lanes, levels)), f32),
-            dma((6,)), dma((2,)), dma, dma((B * C,)), dma((X - 1,)), dma((X - 1,)), dma((2,)),
+            dma((6,)), dma((2,)), dma, dma((B * C,)), dma, dma((2, B * C)), dma, dma((2,)),
             pltpu.SemaphoreType.REGULAR,
         ],
         compiler_params=pltpu.CompilerParams(
-            collective_id=0, has_side_effects=True, vmem_limit_bytes=60 * 2**20
+            collective_id=0, has_side_effects=True, vmem_limit_bytes=40 * 2**20
         ),
         cost_estimate=pl.CostEstimate(flops=10**9, bytes_accessed=10**7, transcendentals=0),
-    )(warming, table, thermal, operator, analysis, order)
+    )(*(pltpu.with_memory_space_constraint(v, pltpu.HBM) for v in operands))
     return jnp.transpose(result.reshape(own_degrees, 2, K, levels), (0, 2, 1, 3))
 
 

time: 53.3 us -> 43.6 us (0.82)
  the two profiles are of different devices: /device:TPU:128 before, /device:TPU:1 now
where the time goes in v4:
time: 43.6 us; the launch traced here: 43.5 us
  Pallas kernels  42.5 us (97%)
  local copies, waits for them, and re-layouts  0.91 us (2%)
    pallas_call x1, Pallas kernels, shards(): pl.pallas_call(functools.partial(kernel, sizes), out_shape=jax.ShapeDtype...  42.5 us
    reshape x1, local copies, waits for them, and re-layouts, shards(): result.reshape(own_degrees, 2, K, levels)  0.91 us

profile of v4, /device:TPU:1, one launch (start us, length us, event | category | flops | bytes accessed | tf_op | source)
XLA Modules:
  0.0 43.5 jit_solution(1109797820515372288)
XLA Ops:
  0.0 42.5 %shard_map.64 = f32[8,32,256]{2,1,0:T(8,128)S(1)} custom-call(bf16[4,96,1536]{2,1,0:T(8,128)(2,1)} %warm_hbm.1, bf16[96,8,128]{2,1,0:T(8,128)(2,1)} %bitcast.6, f32[8,16,2,256]{3,2,1,0:T(2,128)} %thermal_hbm.1, f32[8,256,256]{2,1,0:T(8,128)} %operator_hbm.1, bf16[256,1536]{1,0:T(8,128)(2,1)} %constant.10.analysis_hbm, bf16[512,512]{1,0:T(8,128)(2,1)} %constant.11.order_hbm), custom_call_target="tpu_custom_call" | custom-call | flops 1000000000 | bytes 10000000 | tf_op jit(solution)/shard_map/pallas_call | solution.py:279
  42.6 0.9 %copy.9 = f32[8,2,16,256]{3,1,2,0:T(2,128)} copy(f32[8,2,16,256]{3,2,1,0:T(8,128)S(1)} %bitcast.5) | data formatting | bytes 524288 | tf_op jit(solution)/shard_map/reshape | solution.py:310

commit v5 on v4

--- a/solution.py
+++ b/solution.py
@@ -18,13 +18,13 @@
 def analysis_rows(orders, stride, longitudes):
     phase = (np.arange(orders)[:, None] * stride * np.arange(longitudes)[None, :]) % longitudes
     angles = phase.astype(np.float32) * np.float32(2.0 * math.pi / longitudes)
-    stacked = np.stack([np.cos(angles), -np.sin(angles)], axis=0) / np.float32(longitudes)
+    stacked = np.stack([np.cos(angles), -np.sin(angles)], axis=1) / np.float32(longitudes)
     return jnp.asarray(stacked.reshape(2 * orders, longitudes)).astype(bf16)
 
 
 def level_order(xs, ks, own_levels):
     n = xs * ks * 2 * own_levels
-    x, k, c, r = np.unravel_index(np.arange(n), (xs, ks, 2, own_levels))
+    x, r, k, c = np.unravel_index(np.arange(n), (xs, own_levels, ks, 2))
     matrix = np.zeros((n, n), np.float32)
     matrix[np.arange(n), np.ravel_multi_index((c, x, k, r), (2, xs, ks, own_levels))] = backward_euler_update
     return jnp.asarray(matrix).astype(bf16)
@@ -40,7 +40,7 @@
     warm_hbm, table_hbm, thermal_hbm, operator_hbm, analysis_hbm, order_hbm,
     out_ref,
     warm, table, thermal, operator, analysis, order,
-    rows32, turned32, f_send, f_all, p_send, p_recv, s_send, s_recv, operator16, own_part, ordered32,
+    rows32, turned32, total32, p_rows, f_send, f_all, p_send, p_recv, s_send, s_recv, operator16, own_part, ordered32,
     load_sems, p_sems, f_send_sem, f_sems, x_send_sem, x_recv_sems, far_sem, s_sems, plane_sem,
 ):
     X, Y, A, B, C = sizes
@@ -52,7 +52,7 @@
     me = (b * C + c) * K + k
     own_levels, bands, longitudes = warm.shape
     own_degrees = table.shape[1]
-    lanes = f_send.shape[2]
+    tiles = f_send.shape[1]
 
     def owner(m):
         return {
@@ -89,11 +89,18 @@
 
     loads[0].wait()
     rows32[...] = table[...].astype(f32).reshape(bands * own_degrees, M)
-    for l in range(own_degrees):
-        part = rows32[pl.ds(l, bands, stride=own_degrees), :]
-        part = jnp.concatenate([part, jnp.zeros((lanes - bands, M), f32)], axis=0)
-        turned32[pl.ds(l, M, stride=own_degrees), :] = part.T
-    p_send[...] = turned32[...].reshape(M, own_degrees, lanes).astype(bf16)
+    for half in range(2):
+        wide = jnp.concatenate(
+            [
+                rows32[pl.ds(l, bands, stride=own_degrees), :].T
+                for l in range(half * own_degrees // 2, (half + 1) * own_degrees // 2)
+            ],
+            axis=1,
+        )
+        for tile in range(tiles):
+            turned32[tile, pl.ds(half, M, stride=2), :] = wide[:, tile * 128 : (tile + 1) * 128]
+    for tile in range(tiles):
+        p_send[:, tile] = turned32[tile].reshape(M, 2, 128).astype(bf16)
 
     pl.semaphore_wait(barrier, len(columns) + len(rows) + X - 1)
     for step in rows:
@@ -101,14 +108,14 @@
 
     loads[1].wait()
     loads[2].wait()
-    for r in range(own_levels):
-        part = lax.dot_general(analysis[...], warm[r], NT, preferred_element_type=f32)
-        part = jnp.concatenate([part, jnp.zeros((2 * M, lanes - bands), f32)], axis=1)
-        for half in range(2):
-            turned32[pl.ds(half * own_levels + r, M, stride=2 * own_levels), :] = part[
-                half * M : (half + 1) * M
-            ]
-    f_send[...] = turned32[...].reshape(M, 2 * own_levels, lanes).astype(bf16)
+    fourier = lax.dot_general(
+        analysis[...], warm[...].reshape(own_levels * bands, longitudes), NT,
+        preferred_element_type=f32,
+    )
+    for tile in range(tiles):
+        f_send[:, tile] = (
+            fourier[:, tile * 128 : (tile + 1) * 128].reshape(M, 2, 128).astype(bf16)
+        )
 
     pl.semaphore_wait(plane_sem, len(rows))
 
@@ -190,7 +197,7 @@
             arrived(right, chunk, x_recv_sems.at[1, chunk])
             pass_on(right, chunk, left, far_sem)
 
-    lag = min(5, B * C)
+    lag = min(8, B * C)
     for chunk in range(B * C):
         arrived(x, chunk, f_sems.at[chunk])
         pass_on(x, chunk, right, x_recv_sems.at[0, chunk])
@@ -199,43 +206,66 @@
             hop(chunk - lag)
     for chunk in range(B * C - lag, B * C):
         hop(chunk)
-    for chunk in range(B * C):
-        if chunk < B * C // 2:
-            arrived(right, chunk, x_recv_sems.at[1, chunk])
-        else:
-            arrived(left, chunk, x_recv_sems.at[0, chunk])
+    def spread(buffer, parts):
+        wide = jnp.concatenate(
+            [buffer[:, tile].reshape(2 * K, 128) for tile in range(tiles)], axis=1
+        )
+        return jnp.concatenate(
+            [wide[:, part * bands : (part + 1) * bands] for part in range(parts)], axis=0
+        )
+
+    width = K * 2 * own_levels
+    rows = K * own_degrees
+
+    def spectrum(source):
+        total = jnp.zeros((rows, width), f32)
+        for band in range(B * C):
+            here = pl.ds(band * K, K)
+            total += lax.dot_general(
+                p_rows[band], spread(f_all.at[source, here], own_levels), NT,
+                preferred_element_type=f32,
+            )
+        for l in range(own_degrees // 2):
+            total32[pl.ds(l, 2 * K, stride=own_degrees // 2), :] = total[
+                l * 2 * K : (l + 1) * 2 * K
+            ]
+        s_send[source] = total32[...].reshape(K, own_degrees, width).astype(bf16)
+
+        def send(i, carry):
+            target = lax.rem(k + i, K)
+            pltpu.make_async_remote_copy(
+                src_ref=s_send.at[source, target], dst_ref=s_recv.at[source, k],
+                send_sem=s_sems.at[0], recv_sem=s_sems.at[1],
+                device_id={"y": target // A, "a": lax.rem(target, A)}, device_id_type=MESH,
+            ).start()
+            return carry
+
+        pltpu.make_async_copy(s_send.at[source, k], s_recv.at[source, k], s_sems.at[1]).start()
+        lax.fori_loop(1, K, send, 0)
+
+    pltpu.make_async_copy(p_recv, p_recv, p_sems.at[1]).wait()
+    for band in range(B * C):
+        p_rows[band] = spread(p_recv.at[pl.ds(band * K, K)], own_degrees // 2)
+    spectrum(x)
+    for chunk in range(B * C // 2, B * C):
+        arrived(left, chunk, x_recv_sems.at[0, chunk])
+    spectrum(left)
+    for chunk in range(B * C // 2):
+        arrived(right, chunk, x_recv_sems.at[1, chunk])
+    spectrum(right)
     pltpu.make_async_copy(f_all.at[far], f_all.at[far], far_sem).wait()
-    pltpu.make_async_copy(p_recv, p_recv, p_sems.at[1]).wait()
-
-    width = X * K * 2 * own_levels
-    total = jnp.zeros((K * own_degrees, width), f32)
-    for band in range(B * C):
-        here = pl.ds(band * K, K)
-        total += lax.dot_general(
-            p_recv[here].reshape(K * own_degrees, lanes),
-            f_all[:, here].reshape(width, lanes),
-            NT, preferred_element_type=f32,
-        )
-    s_send[...] = total.reshape(K, own_degrees, width).astype(bf16)
-
-    def send_s(i, carry):
-        target = lax.rem(k + i, K)
-        pltpu.make_async_remote_copy(
-            src_ref=s_send.at[target], dst_ref=s_recv.at[k],
-            send_sem=s_sems.at[0], recv_sem=s_sems.at[1],
-            device_id={"y": target // A, "a": lax.rem(target, A)}, device_id_type=MESH,
-        ).start()
-        return carry
-
-    pltpu.make_async_copy(s_send.at[k], s_recv.at[k], s_sems.at[1]).start()
-    lax.fori_loop(1, K, send_s, 0)
+    spectrum(far)
     pltpu.make_async_copy(s_recv, s_recv, s_sems.at[1]).wait()
 
-    half = width // 2
-    ordered = jnp.dot(
-        s_recv[...].reshape(K * own_degrees, width), order[...], preferred_element_type=f32
-    )
-    rows, wide = K * own_degrees, ordered32.shape[1]
+    half = X * K * own_levels
+    ordered = jnp.zeros((rows, 2 * half), f32)
+    for source in range(X):
+        ordered += jnp.dot(
+            s_recv[source].reshape(rows, width),
+            order[source * width : (source + 1) * width],
+            preferred_element_type=f32,
+        )
+    wide = ordered32.shape[1]
     pieces = 2 * half // wide
     for piece in range(pieces):
         ordered32[piece * rows : (piece + 1) * rows] = ordered[:, piece * wide : (piece + 1) * wide]
@@ -256,9 +286,11 @@
 
     for _ in range(X - 1):
         pltpu.make_async_copy(f_all.at[x], f_all.at[x], x_send_sem).wait()
-    for buffer, sem in ((f_send, f_send_sem), (p_send, p_sems.at[0]), (s_send, s_sems.at[0])):
-        sent = buffer.at[pl.ds(0, buffer.shape[0] - 1)]
+    for buffer, sem in ((f_send, f_send_sem), (p_send, p_sems.at[0])):
+        sent = buffer.at[pl.ds(0, M - 1)]
         pltpu.make_async_copy(sent, sent, sem).wait()
+    sent = s_send.at[:, pl.ds(0, K - 1)]
+    pltpu.make_async_copy(sent, sent, s_sems.at[0]).wait()
 
 
 def shards(sizes, warming, table, thermal, operator):
@@ -270,6 +302,7 @@
     degrees = own_degrees * X * K
     levels = thermal.shape[3]
     lanes = 128
+    tiles = own_levels * bands // lanes
     vmem = pltpu.VMEM
     dma = pltpu.SemaphoreType.DMA
     table = jnp.transpose(table, (1, 2, 0))
@@ -289,13 +322,15 @@
             vmem(analysis.shape, bf16),
             vmem(order.shape, bf16),
             vmem((bands * own_degrees, M), f32),
-            vmem((M * own_degrees, lanes), f32),
-            vmem((M, 2 * own_levels, lanes), bf16),
-            vmem((X, M, 2 * own_levels, lanes), bf16),
-            vmem((M, own_degrees, lanes), bf16),
-            vmem((M, own_degrees, lanes), bf16),
-            vmem((K, own_degrees, 2 * levels), bf16),
-            vmem((K, own_degrees, 2 * levels), bf16),
+            vmem((tiles, 2 * M, lanes), f32),
+            vmem((K * own_degrees, 2 * levels // X), f32),
+            vmem((B * C, K * own_degrees, bands), bf16),
+            vmem((M, tiles, 2, lanes), bf16),
+            vmem((X, M, tiles, 2, lanes), bf16),
+            vmem((M, tiles, 2, lanes), bf16),
+            vmem((M, tiles, 2, lanes), bf16),
+            vmem((X, K, own_degrees, 2 * levels // X), bf16),
+            vmem((X, K, own_degrees, 2 * levels // X), bf16),
             vmem(operator.shape, bf16),
             vmem((own_degrees, 2 * K, levels), f32),
             vmem((2 * levels // min(lanes, levels) * K * own_degrees, min(lanes, levels)), f32),

time: 43.6 us -> 41.5 us (0.952)
  Pallas kernels: 42.5 us -> 40.4 us
    pallas_call x1, Pallas kernels: 42.5 us -> 40.4 us  [shards(): pl.pallas_call(functools.partial(kernel, sizes), out_shape=jax.ShapeDtype...]
where the time goes in v5:
time: 41.5 us; the launch traced here: 41.4 us
  Pallas kernels  40.4 us (97%)
  local copies, waits for them, and re-layouts  0.91 us (2%)
    pallas_call x1, Pallas kernels, shards(): pl.pallas_call(functools.partial(kernel, sizes), out_shape=jax.ShapeDtype...  40.4 us
    reshape x1, local copies, waits for them, and re-layouts, shards(): result.reshape(own_degrees, 2, K, levels)  0.91 us

profile of v5, /device:TPU:1, one launch (start us, length us, event | category | flops | bytes accessed | tf_op | source)
XLA Modules:
  0.0 41.4 jit_solution(8269422661639921919)
XLA Ops:
  0.0 40.4 %shard_map.64 = f32[8,32,256]{2,1,0:T(8,128)S(1)} custom-call(bf16[4,96,1536]{2,1,0:T(8,128)(2,1)} %warm_hbm.1, bf16[96,8,128]{2,1,0:T(8,128)(2,1)} %bitcast.6, f32[8,16,2,256]{3,2,1,0:T(2,128)} %thermal_hbm.1, f32[8,256,256]{2,1,0:T(8,128)} %operator_hbm.1, bf16[256,1536]{1,0:T(8,128)(2,1)} %constant.10.analysis_hbm, bf16[512,512]{1,0:T(8,128)(2,1)} %constant.11.order_hbm), custom_call_target="tpu_custom_call" | custom-call | flops 1000000000 | bytes 10000000 | tf_op jit(solution)/shard_map/pallas_call | solution.py:312
  40.5 0.9 %copy.9 = f32[8,2,16,256]{3,1,2,0:T(2,128)} copy(f32[8,2,16,256]{3,2,1,0:T(8,128)S(1)} %bitcast.5) | data formatting | bytes 524288 | tf_op jit(solution)/shard_map/reshape | solution.py:345

commit v6 on v5

--- a/solution.py
+++ b/solution.py
@@ -40,8 +40,8 @@
     warm_hbm, table_hbm, thermal_hbm, operator_hbm, analysis_hbm, order_hbm,
     out_ref,
     warm, table, thermal, operator, analysis, order,
-    rows32, turned32, total32, p_rows, f_send, f_all, p_send, p_recv, s_send, s_recv, operator16, own_part, ordered32,
-    load_sems, p_sems, f_send_sem, f_sems, x_send_sem, x_recv_sems, far_sem, s_sems, plane_sem,
+    rows32, turned32, total32, p_rows, f_send, f_pair, f_all, p_send, p_pair, p_recv, s_send, s_recv, operator16, own_part, ordered32,
+    load_sems, f_pair_sems, p_pair_sems, p_sems, f_send_sem, f_sems, x_send_sem, x_recv_sems, far_sem, s_sems, plane_sem,
 ):
     X, Y, A, B, C = sizes
     K = Y * A
@@ -49,16 +49,9 @@
     x, y, a = lax.axis_index("x"), lax.axis_index("y"), lax.axis_index("a")
     b, c = lax.axis_index("b"), lax.axis_index("c")
     k = y * A + a
-    me = (b * C + c) * K + k
     own_levels, bands, longitudes = warm.shape
     own_degrees = table.shape[1]
-    tiles = f_send.shape[1]
-
-    def owner(m):
-        return {
-            "b": m // (C * K), "c": lax.rem(m // K, C),
-            "y": lax.rem(m, K) // A, "a": lax.rem(m, A),
-        }
+    tiles = f_send.shape[3]
 
     loads = [
         pltpu.make_async_copy(src, dst, load_sems.at[i])
@@ -80,6 +73,8 @@
 
     columns = [(0, da, db, dc) for da in range(A) for db in range(B) for dc in range(C)][1:]
     rows = [(dy, 0, 0, 0) for dy in range(1, Y)]
+    columns.sort(key=lambda step: -min(A * step[2] + step[1], A * B - A * step[2] - step[1]))
+    rows.sort(key=lambda step: -min(step[0], Y - step[0]))
     for step in columns + rows:
         pl.semaphore_signal(barrier, inc=1, device_id=plane(*step), device_id_type=MESH)
     for d in range(1, X):
@@ -100,11 +95,23 @@
         for tile in range(tiles):
             turned32[tile, pl.ds(half, M, stride=2), :] = wide[:, tile * 128 : (tile + 1) * 128]
     for tile in range(tiles):
-        p_send[:, tile] = turned32[tile].reshape(M, 2, 128).astype(bf16)
+        p_send[:, :, :, tile] = turned32[tile].reshape(B, C, K, 2, 128).astype(bf16)
 
     pl.semaphore_wait(barrier, len(columns) + len(rows) + X - 1)
     for step in rows:
         pl.semaphore_signal(plane_sem, inc=1, device_id=plane(*step), device_id_type=MESH)
+
+    def pair(own, both, sems):
+        for other in range(1, C):
+            core = lax.rem(c + other, C)
+            pltpu.make_async_remote_copy(
+                src_ref=own.at[:, core], dst_ref=both.at[:, :, c],
+                send_sem=sems.at[0], recv_sem=sems.at[1],
+                device_id={"c": core}, device_id_type=MESH,
+            ).start()
+        pltpu.make_async_copy(own.at[:, c], both.at[:, :, c], sems.at[1]).start()
+
+    pair(p_send, p_pair, p_pair_sems)
 
     loads[1].wait()
     loads[2].wait()
@@ -113,50 +120,51 @@
         preferred_element_type=f32,
     )
     for tile in range(tiles):
-        f_send[:, tile] = (
-            fourier[:, tile * 128 : (tile + 1) * 128].reshape(M, 2, 128).astype(bf16)
-        )
-
+        f_send[:, :, :, tile] = (
+            fourier[:, tile * 128 : (tile + 1) * 128].reshape(B, C, K, 2, 128).astype(bf16)
+        )
+
+    pair(f_send, f_pair, f_pair_sems)
     pl.semaphore_wait(plane_sem, len(rows))
 
-    def f_copy(m, chunk):
+    def f_copy(target_b, target_k, chunk):
         return pltpu.make_async_remote_copy(
-            src_ref=f_send.at[m], dst_ref=f_all.at[x, me],
+            src_ref=f_pair.at[target_b, target_k], dst_ref=f_all.at[x, b, k],
             send_sem=f_send_sem, recv_sem=f_sems.at[chunk],
-            device_id=owner(m), device_id_type=MESH,
-        )
-
-    def p_copy(m, chunk):
+            device_id={"y": target_k // A, "a": lax.rem(target_k, A), "b": target_b},
+            device_id_type=MESH,
+        )
+
+    def p_copy(target_b, target_k, chunk):
         return pltpu.make_async_remote_copy(
-            src_ref=p_send.at[m], dst_ref=p_recv.at[me],
+            src_ref=p_pair.at[target_b, target_k], dst_ref=p_recv.at[b, k],
             send_sem=p_sems.at[0], recv_sem=p_sems.at[1],
-            device_id=owner(m), device_id_type=MESH,
-        )
-
-    chunks = sorted(
-        ((db, dc) for db in range(B) for dc in range(C)),
-        key=lambda step: min(step[0], B - step[0]),
-    )
-
-    def band_at(sign, chunk):
-        db, dc = chunks[chunk]
-        return lax.rem(b + sign * db + B, B) * C + lax.rem(c + sign * dc + C, C)
-
-    def send_band(copy, chunk):
-        band = band_at(1, chunk)
+            device_id={"y": target_k // A, "a": lax.rem(target_k, A), "b": target_b},
+            device_id_type=MESH,
+        )
+
+    chunks = sorted(range(B), key=lambda step: min(step, B - step))
+
+    def place(sign, chunk):
+        return lax.rem(b + sign * chunks[chunk] + B, B)
+
+    def send_chunk(copy, chunk):
+        target_b = place(1, chunk)
 
         def send(i, carry):
-            copy(band * K + lax.rem(k + i, K), chunk).start()
+            copy(target_b, lax.rem(k + i, K), chunk).start()
             return carry
 
         lax.fori_loop(1 if chunk == 0 else 0, K, send, 0)
 
-    pltpu.make_async_copy(f_send.at[me], f_all.at[x, me], f_sems.at[0]).start()
-    for chunk in range(B * C):
-        send_band(f_copy, chunk)
-    pltpu.make_async_copy(p_send.at[me], p_recv.at[me], p_sems.at[1]).start()
-    for chunk in range(B * C):
-        send_band(p_copy, chunk)
+    pltpu.make_async_copy(f_pair, f_pair, f_pair_sems.at[1]).wait()
+    pltpu.make_async_copy(f_pair.at[b, k], f_all.at[x, b, k], f_sems.at[0]).start()
+    for chunk in range(B):
+        send_chunk(f_copy, chunk)
+    pltpu.make_async_copy(p_pair, p_pair, p_pair_sems.at[1]).wait()
+    pltpu.make_async_copy(p_pair.at[b, k], p_recv.at[b, k], p_sems.at[1]).start()
+    for chunk in range(B):
+        send_chunk(p_copy, chunk)
 
     loads[3].wait()
     loads[4].wait()
@@ -177,7 +185,7 @@
     far = lax.rem(x + 2, X)
 
     def block(source, chunk):
-        return f_all.at[source, pl.ds(band_at(-1, chunk) * K, K)]
+        return f_all.at[source, place(-1, chunk)]
 
     def pass_on(source, chunk, target, sem):
         pltpu.make_async_remote_copy(
@@ -189,26 +197,15 @@
     def arrived(source, chunk, sem):
         pltpu.make_async_copy(block(source, chunk), block(source, chunk), sem).wait()
 
-    def hop(chunk):
-        if chunk < B * C // 2:
-            arrived(left, chunk, x_recv_sems.at[0, chunk])
-            pass_on(left, chunk, right, far_sem)
-        else:
-            arrived(right, chunk, x_recv_sems.at[1, chunk])
-            pass_on(right, chunk, left, far_sem)
-
-    lag = min(8, B * C)
-    for chunk in range(B * C):
+    for chunk in range(B):
         arrived(x, chunk, f_sems.at[chunk])
         pass_on(x, chunk, right, x_recv_sems.at[0, chunk])
         pass_on(x, chunk, left, x_recv_sems.at[1, chunk])
-        if chunk >= lag:
-            hop(chunk - lag)
-    for chunk in range(B * C - lag, B * C):
-        hop(chunk)
-    def spread(buffer, parts):
+        pass_on(x, chunk, far, far_sem)
+
+    def spread(buffer, core, parts):
         wide = jnp.concatenate(
-            [buffer[:, tile].reshape(2 * K, 128) for tile in range(tiles)], axis=1
+            [buffer[:, core, tile].reshape(2 * K, 128) for tile in range(tiles)], axis=1
         )
         return jnp.concatenate(
             [wide[:, part * bands : (part + 1) * bands] for part in range(parts)], axis=0
@@ -220,9 +217,8 @@
     def spectrum(source):
         total = jnp.zeros((rows, width), f32)
         for band in range(B * C):
-            here = pl.ds(band * K, K)
             total += lax.dot_general(
-                p_rows[band], spread(f_all.at[source, here], own_levels), NT,
+                p_rows[band], spread(f_all.at[source, band // C], band % C, own_levels), NT,
                 preferred_element_type=f32,
             )
         for l in range(own_degrees // 2):
@@ -245,12 +241,12 @@
 
     pltpu.make_async_copy(p_recv, p_recv, p_sems.at[1]).wait()
     for band in range(B * C):
-        p_rows[band] = spread(p_recv.at[pl.ds(band * K, K)], own_degrees // 2)
+        p_rows[band] = spread(p_recv.at[band // C], band % C, own_degrees // 2)
     spectrum(x)
-    for chunk in range(B * C // 2, B * C):
+    for chunk in range(B):
         arrived(left, chunk, x_recv_sems.at[0, chunk])
     spectrum(left)
-    for chunk in range(B * C // 2):
+    for chunk in range(B):
         arrived(right, chunk, x_recv_sems.at[1, chunk])
     spectrum(right)
     pltpu.make_async_copy(f_all.at[far], f_all.at[far], far_sem).wait()
@@ -286,9 +282,14 @@
 
     for _ in range(X - 1):
         pltpu.make_async_copy(f_all.at[x], f_all.at[x], x_send_sem).wait()
-    for buffer, sem in ((f_send, f_send_sem), (p_send, p_sems.at[0])):
-        sent = buffer.at[pl.ds(0, M - 1)]
+    for both, sem in ((f_pair, f_send_sem), (p_pair, p_sems.at[0])):
+        sent = both.at[:, pl.ds(0, K - 1)]
         pltpu.make_async_copy(sent, sent, sem).wait()
+        sent = both.at[pl.ds(0, B - 1), K - 1]
+        pltpu.make_async_copy(sent, sent, sem).wait()
+    for own, sems in ((f_send, f_pair_sems), (p_send, p_pair_sems)):
+        sent = own.at[:, pl.ds(0, C - 1)]
+        pltpu.make_async_copy(sent, sent, sems.at[0]).wait()
     sent = s_send.at[:, pl.ds(0, K - 1)]
     pltpu.make_async_copy(sent, sent, s_sems.at[0]).wait()
 
@@ -325,16 +326,18 @@
             vmem((tiles, 2 * M, lanes), f32),
             vmem((K * own_degrees, 2 * levels // X), f32),
             vmem((B * C, K * own_degrees, bands), bf16),
-            vmem((M, tiles, 2, lanes), bf16),
-            vmem((X, M, tiles, 2, lanes), bf16),
-            vmem((M, tiles, 2, lanes), bf16),
-            vmem((M, tiles, 2, lanes), bf16),
+            vmem((B, C, K, tiles, 2, lanes), bf16),
+            vmem((B, K, C, tiles, 2, lanes), bf16),
+            vmem((X, B, K, C, tiles, 2, lanes), bf16),
+            vmem((B, C, K, tiles, 2, lanes), bf16),
+            vmem((B, K, C, tiles, 2, lanes), bf16),
+            vmem((B, K, C, tiles, 2, lanes), bf16),
             vmem((X, K, own_degrees, 2 * levels // X), bf16),
             vmem((X, K, own_degrees, 2 * levels // X), bf16),
             vmem(operator.shape, bf16),
             vmem((own_degrees, 2 * K, levels), f32),
             vmem((2 * levels // min(lanes, levels) * K * own_degrees, min(lanes, levels)), f32),
-            dma((6,)), dma((2,)), dma, dma((B * C,)), dma, dma((2, B * C)), dma, dma((2,)),
+            dma((6,)), dma((2,)), dma((2,)), dma((2,)), dma, dma((B,)), dma, dma((2, B)), dma, dma((2,)),
             pltpu.SemaphoreType.REGULAR,
         ],
         compiler_params=pltpu.CompilerParams(

time: 41.5 us -> 41.4 us (level)
  the two profiles are of different devices: /device:TPU:1 before, /device:TPU:8 now
where the time goes in v6:
time: 41.4 us; the launch traced here: 41.3 us
  Pallas kernels  40.3 us (97%)
  local copies, waits for them, and re-layouts  0.91 us (2%)
    pallas_call x1, Pallas kernels, shards(): pl.pallas_call(functools.partial(kernel, sizes), out_shape=jax.ShapeDtype...  40.3 us
    reshape x1, local copies, waits for them, and re-layouts, shards(): result.reshape(own_degrees, 2, K, levels)  0.91 us

profile of v6, /device:TPU:8, one launch (start us, length us, event | category | flops | bytes accessed | tf_op | source)
XLA Modules:
  0.0 41.3 jit_solution(5753621908731486147)
XLA Ops:
  0.0 40.3 %shard_map.64 = f32[8,32,256]{2,1,0:T(8,128)S(1)} custom-call(bf16[4,96,1536]{2,1,0:T(8,128)(2,1)} %warm_hbm.1, bf16[96,8,128]{2,1,0:T(8,128)(2,1)} %bitcast.6, f32[8,16,2,256]{3,2,1,0:T(2,128)} %thermal_hbm.1, f32[8,256,256]{2,1,0:T(8,128)} %operator_hbm.1, bf16[256,1536]{1,0:T(8,128)(2,1)} %constant.10.analysis_hbm, bf16[512,512]{1,0:T(8,128)(2,1)} %constant.11.order_hbm), custom_call_target="tpu_custom_call" | custom-call | flops 1000000000 | bytes 10000000 | tf_op jit(solution)/shard_map/pallas_call | solution.py:313
  40.4 0.9 %copy.9 = f32[8,2,16,256]{3,1,2,0:T(2,128)} copy(f32[8,2,16,256]{3,2,1,0:T(8,128)S(1)} %bitcast.5) | data formatting | bytes 524288 | tf_op jit(solution)/shard_map/reshape | solution.py:348

commit v7 on v6

--- a/solution.py
+++ b/solution.py
@@ -231,12 +231,12 @@
             target = lax.rem(k + i, K)
             pltpu.make_async_remote_copy(
                 src_ref=s_send.at[source, target], dst_ref=s_recv.at[source, k],
-                send_sem=s_sems.at[0], recv_sem=s_sems.at[1],
+                send_sem=s_sems.at[0], recv_sem=s_sems.at[1 + source],
                 device_id={"y": target // A, "a": lax.rem(target, A)}, device_id_type=MESH,
             ).start()
             return carry
 
-        pltpu.make_async_copy(s_send.at[source, k], s_recv.at[source, k], s_sems.at[1]).start()
+        pltpu.make_async_copy(s_send.at[source, k], s_recv.at[source, k], s_sems.at[1 + source]).start()
         lax.fori_loop(1, K, send, 0)
 
     pltpu.make_async_copy(p_recv, p_recv, p_sems.at[1]).wait()
@@ -251,14 +251,15 @@
     spectrum(right)
     pltpu.make_async_copy(f_all.at[far], f_all.at[far], far_sem).wait()
     spectrum(far)
-    pltpu.make_async_copy(s_recv, s_recv, s_sems.at[1]).wait()
 
     half = X * K * own_levels
     ordered = jnp.zeros((rows, 2 * half), f32)
-    for source in range(X):
+    for source in (x, left, right, far):
+        landed = s_recv.at[source]
+        pltpu.make_async_copy(landed, landed, s_sems.at[1 + source]).wait()
         ordered += jnp.dot(
             s_recv[source].reshape(rows, width),
-            order[source * width : (source + 1) * width],
+            order[pl.ds(pl.multiple_of(source * width, width), width), :],
             preferred_element_type=f32,
         )
     wide = ordered32.shape[1]
@@ -337,7 +338,7 @@
             vmem(operator.shape, bf16),
             vmem((own_degrees, 2 * K, levels), f32),
             vmem((2 * levels // min(lanes, levels) * K * own_degrees, min(lanes, levels)), f32),
-            dma((6,)), dma((2,)), dma((2,)), dma((2,)), dma, dma((B,)), dma, dma((2, B)), dma, dma((2,)),
+            dma((6,)), dma((2,)), dma((2,)), dma((2,)), dma, dma((B,)), dma, dma((2, B)), dma, dma((1 + X,)),
             pltpu.SemaphoreType.REGULAR,
         ],
         compiler_params=pltpu.CompilerParams(

time: 41.4 us -> 41.3 us (level)
  no operation moved by 1% of the time
where the time goes in v7:
time: 41.3 us; the launch traced here: 41.2 us
  Pallas kernels  40.2 us (97%)
  local copies, waits for them, and re-layouts  0.91 us (2%)
    pallas_call x1, Pallas kernels, shards(): pl.pallas_call(functools.partial(kernel, sizes), out_shape=jax.ShapeDtype...  40.2 us
    reshape x1, local copies, waits for them, and re-layouts, shards(): result.reshape(own_degrees, 2, K, levels)  0.91 us

profile of v7, /device:TPU:8, one launch (start us, length us, event | category | flops | bytes accessed | tf_op | source)
XLA Modules:
  0.0 41.2 jit_solution(14730473561901456408)
XLA Ops:
  0.0 40.2 %shard_map.64 = f32[8,32,256]{2,1,0:T(8,128)S(1)} custom-call(bf16[4,96,1536]{2,1,0:T(8,128)(2,1)} %warm_hbm.1, bf16[96,8,128]{2,1,0:T(8,128)(2,1)} %bitcast.6, f32[8,16,2,256]{3,2,1,0:T(2,128)} %thermal_hbm.1, f32[8,256,256]{2,1,0:T(8,128)} %operator_hbm.1, bf16[256,1536]{1,0:T(8,128)(2,1)} %constant.10.analysis_hbm, bf16[512,512]{1,0:T(8,128)(2,1)} %constant.11.order_hbm), custom_call_target="tpu_custom_call" | custom-call | flops 1000000000 | bytes 10000000 | tf_op jit(solution)/shard_map/pallas_call | solution.py:314
  40.2 0.9 %copy.9 = f32[8,2,16,256]{3,1,2,0:T(2,128)} copy(f32[8,2,16,256]{3,2,1,0:T(8,128)S(1)} %bitcast.5) | data formatting | bytes 524288 | tf_op jit(solution)/shard_map/reshape | solution.py:349
